TPU v7x, 256 devices: a whole 4x4x8 slice. The times are simulated.
256 devices in a mesh: row: 16 (over x_lo, z), rep: 8 (over x_hi, y), feat: 2 (over core).
Axes of the slice: x: 4 (x_hi: 2, x_lo: 2; x = x_hi * 2 + x_lo), y: 4, z: 8, core: 2. Of those that a mesh axis runs over, the one named last changes fastest.
Arguments:
- features: bfloat16 [32768, 512], P('row', 'feat'), may hold values from -6 to 6
- grad_out: bfloat16 [32768, 512], P('row', 'feat'), may hold values from -6 to 6
- relu_mask: int32 [32768, 512], P('row', 'feat'), may hold values 0 or 1
- block_columns: int32 [256, 128], P('row', 'rep'), may hold values from 0 to 255, as said below
- block_count: int32 [256], P('row'), may hold values from 1 to 128, as said below
- block_weights: bfloat16 [256, 128, 128, 128], P('row', 'rep'), may hold values from -0.0625 to 0.0625
- self_weight: bfloat16 [512, 512], P('feat'), may hold values from -0.25 to 0.25
- neighbor_weight: bfloat16 [512, 512], P('feat'), may hold values from -0.25 to 0.25
Outputs:
- features_grad: float32 [32768, 512], P(('row', 'rep'), 'feat')
- self_grad: float32 [512, 512], P('feat')
- neighbor_grad: float32 [512, 512], P('feat')
Inputs may be any that keep to these rules, and one draw needn't show every extreme that they name: block_columns[b, k] is a block of the index of row that holds block row b, or of the index just before or just after it, the last index of row and the first being neighbours; each index of row holds 16 consecutive blocks. Block row b uses slots 0 to block_count[b] - 1; the other slots are ignored.
All inputs are finite; a program needn't handle non-finite values. No bound on the sum of `relu_mask` on one device may be relied on, other than what follows from the above.
Results may differ from a plain program's by a relative error of at most 0.0034.
Values may be sent and summed in bfloat16 or wider, within the bound.
No kernel may reach another device: no remote copies, remote signals or barrier semaphores. Data moves between devices by JAX's collectives and lax.ppermute only.
A program may use at most 192 MiB of HBM per device.

v0:
```python
import jax
import jax.numpy as jnp
from jax import lax
from jax.sharding import PartitionSpec as P


def extended_2(block, sides, width):
    for axis, dim in sides:
        count = lax.axis_size(axis)
        forward = [(i, i + 1) for i in range(count - 1)]
        forward.append((count - 1, 0))
        backward = [(target, source) for source, target in forward]
        low = lax.ppermute(
            lax.slice_in_dim(block, block.shape[dim] - width, None, axis=dim), axis, forward
        )
        high = lax.ppermute(lax.slice_in_dim(block, 0, width, axis=dim), axis, backward)
        block = jnp.concatenate([low, block, high], axis=dim)
    return block


def shifted(array, axis, by):
    size = lax.axis_size(axis)
    return lax.ppermute(array, axis, [(i, (i + by) % size) for i in range(size)])


def local(
    features,
    grad_out,
    relu_mask,
    block_columns,
    block_count,
    block_weights,
    self_weight,
    neighbor_weight,
):
    row_devices = lax.axis_size("row")
    rep_devices = lax.axis_size("rep")
    row_index = lax.axis_index("row")
    rep_index = lax.axis_index("rep")
    local_blocks, slot_width = block_columns.shape
    block_size = block_weights.shape[2]
    row_count, half_width = features.shape
    share_rows = row_count // rep_devices
    slot_count = local_blocks * slot_width
    share_start = rep_index * share_rows
    slot_number = rep_index * slot_width + jnp.arange(slot_width, dtype=jnp.int32)
    live_slots = slot_number[None, :] < block_count[:, None]
    masked_vals = jnp.where(
        live_slots[:, :, None, None], block_weights, jnp.zeros_like(block_weights)
    )
    relative = (block_columns // local_blocks - row_index) % row_devices
    neighbour_side = jnp.where(relative == row_devices - 1, 0, jnp.where(relative == 0, 1, 2))
    positions = (neighbour_side * local_blocks + block_columns % local_blocks).reshape(slot_count)
    extended = extended_2(features, (("row", 0),), row_count)
    sources = extended.reshape(3 * local_blocks, block_size, half_width)[positions]
    products = jnp.einsum(
        "sij,sjd->sid",
        masked_vals.reshape(slot_count, block_size, block_size),
        sources,
        preferred_element_type=jnp.float32,
    )
    partial_sums = (
        products.reshape(local_blocks, slot_width, block_size, half_width)
        .sum(axis=1)
        .reshape(row_count, half_width)
    )
    masked_grad = grad_out * relu_mask.astype(jnp.bfloat16)
    grad_full = lax.all_gather(masked_grad, "feat", axis=1, tiled=True)
    scaling = float(row_count * row_devices) ** (-0.5)
    aggregate = lax.psum(partial_sums, "rep").astype(jnp.bfloat16)
    weight_terms = (
        jnp.einsum("rd,ro->do", features, grad_full, preferred_element_type=jnp.float32),
        jnp.einsum("rd,ro->do", aggregate, grad_full, preferred_element_type=jnp.float32),
    )
    self_sum, neighbor_sum = lax.psum((weight_terms[0], weight_terms[1]), "row")
    self_grad = self_sum * scaling
    neighbor_grad = neighbor_sum * scaling
    grad_rows = lax.dynamic_slice_in_dim(grad_full, share_start, share_rows, 0)
    self_term = jnp.einsum("ro,do->rd", grad_rows, self_weight, preferred_element_type=jnp.float32)
    neighbor_term = jnp.einsum(
        "ro,do->rd", grad_full, neighbor_weight, preferred_element_type=jnp.float32
    ).astype(jnp.bfloat16)
    contributions = jnp.einsum(
        "bkij,bid->bkjd",
        masked_vals,
        neighbor_term.reshape(local_blocks, block_size, half_width),
        preferred_element_type=jnp.float32,
    )
    contributions = contributions.reshape(slot_count, block_size, half_width)
    destined = jax.ops.segment_sum(contributions, positions, num_segments=3 * local_blocks).reshape(
        3, row_count, half_width
    )
    to_lower = destined[0]
    own_terms = destined[1]
    to_upper = destined[2]
    from_upper = shifted(to_lower, "row", -1)
    from_lower = shifted(to_upper.astype(jnp.bfloat16), "row", 1).astype(to_upper.dtype)
    summed = own_terms + from_upper + from_lower
    returned = lax.psum_scatter(summed, "rep", scatter_dimension=0, tiled=True)
    features_grad = self_term + returned
    return (features_grad, self_grad, neighbor_grad)


def solution(mesh):
    return jax.shard_map(
        local,
        mesh=mesh,
        in_specs=(
            P("row", "feat"),
            P("row", "feat"),
            P("row", "feat"),
            P("row", "rep"),
            P("row"),
            P("row", "rep", None, None),
            P("feat", None),
            P("feat", None),
        ),
        out_specs=(P(("row", "rep"), "feat"), P("feat", None), P("feat", None)),
        check_vma=False,
    )
```

profile of v0, /device:TPU:33, one launch (start us, length us, event | category | flops | bytes accessed | tf_op | source)
XLA Modules:
  0.0 520.0 jit_solution(4563989208106720826)
XLA Ops:
  7.2 0.0 copy-start
  7.2 0.0 copy-start.7
  7.2 0.0 copy-start.8
  7.2 0.0 all-gather.2.cloned.1.call-start
  7.2 1.7 collective-permute-start.2
  9.0 0.0 collective-permute-start.3
  9.0 3.0 convert_multiply_fusion
  12.0 0.0 all-gather.2.cloned.1.call-update
  12.0 0.0 all-reduce.4.cloned.1.call-start
  12.1 0.0 copy-done.7
  12.1 0.1 reshape.109
  12.2 0.1 broadcast_in_dim_reshape.3
  12.3 0.0 copy-done.8
  12.3 0.1 broadcast_compare_fusion
  12.4 7.3 %broadcast_select_fusion = bf16[16,16,128,128]{3,2,1,0:T(8,128)(2,1)} fusion(bf16[16,16,128,128]{3,2,1,0:T(8,128)(2,1)} %param.13, pred[16,16]{1,0:T(8,128)(4,1)S(1)} %broadcast_compare_fusion), kind=kLoop, calls=%fused_computation.3 | loop fusion | flops 4194304 | bytes 16777472 | tf_op jit(solution)/shard_map/jit(_where)/select_n | solution.py:48
  19.7 11.9 %collective-permute-done.2 = bf16[2048,256]{1,0:T(8,128)(2,1)S(1)} collective-permute-done((bf16[2048,256]{1,0:T(8,128)(2,1)}, bf16[2048,256]{1,0:T(8,128)(2,1)S(1)}, u32[]{:S(2)}, u32[]{:S(2)}) %collective-permute-start.2) | collective-permute-done | bytes 1048608 | tf_op jit(solution)/shard_map/ppermute | solution.py:13
  31.7 1.0 copy-done.5
  32.7 0.8 collective-permute-done.3
  33.4 1.8 pad_maximum_fusion
  35.2 9.8 %gather_fusion = bf16[256,128,256]{2,1,0:T(8,128)(2,1)} fusion(bf16[48,128,256]{2,1,0:T(8,128)(2,1)S(1)} %bitcast.32, s32[1024]{0:T(1024)S(1)} %pad_clamp_fusion), kind=kCustom, calls=%fused_computation | custom fusion | bytes 33555456 | tf_op jit(solution)/shard_map/gather | solution.py:55
  45.0 12.0 %bitcast_reduce_fusion = f32[16,128,256]{2,1,0:T(8,128)} fusion(bf16[256,128,128]{2,1,0:T(8,128)(2,1)} %bitcast.33, bf16[256,128,256]{2,1,0:T(8,128)(2,1)} %gather_fusion), kind=kOutput, calls=%fused_computation.2 | convolution fusion | flops 2155347968 | bytes 27262976 | tf_op jit(solution)/shard_map/sij,sjd->sid/dot_general | solution.py:56
  57.1 2.3 convolution_convert_fusion
  59.4 15.3 %fusion.11 = f32[16,16,128,256]{3,2,1,0:T(8,128)} fusion(bf16[16,16,128,128]{3,2,1,0:T(8,128)(2,1)} %broadcast_select_fusion, bf16[16,128,256,1]{2,1,3,0:T(8,128)(2,1)S(1)} %bitcast.35), kind=kOutput, calls=%fused_computation.36 | convolution fusion | flops 2147483648 | bytes 42991616 | tf_op jit(solution)/shard_map/bkij,bid->bkjd/dot_general | solution.py:83
  74.7 3.4 broadcast_in_dim.26
  78.1 75.1 %scatter_fusion = f32[48,128,256]{2,1,0:T(8,128)} fusion(f32[48,128,256]{2,1,0:T(8,128)} %broadcast_in_dim.26, s32[256]{0:T(256)S(1)} %reshape.109, f32[256,128,256]{2,1,0:T(8,128)} %bitcast.31), kind=kCustom, calls=%fused_computation.1 | custom fusion | flops 8388608 | bytes 100664320 | tf_op jit(solution)/shard_map/scatter-add | solution.py:90
  153.2 2.7 slice.22
  155.9 4.9 fusion.10
  160.8 2.9 collective-permute-start.1
  163.6 1.1 collective-permute-start
  164.8 74.4 %all-reduce.5 = bf16[2048,256]{1,0:T(8,128)(2,1)} all-reduce(f32[2048,256]{1,0:T(8,128)} %bitcast.34), channel_id=1, replica_groups=mesh['row'=16,'rep'=8,'feat'=2] {'rep'}, use_global_device_ids=true, to_apply=%region_4.5 | all-reduce | flops 524288 | bytes 3145728 | tf_op jit(solution)/shard_map/psum | solution.py:70
  239.1 0.0 copy-done.4
  239.1 1.5 convolution_bitcast_fusion
  240.7 2.9 fusion.12
  243.6 0.0 all-reduce.4.cloned.1.call-update
  243.6 0.0 reduce-scatter.2.cloned.1.call-start
  243.7 0.0 collective-permute-done.1
  243.7 0.0 collective-permute-done
  243.7 0.0 copy-start.6
  243.7 0.0 copy-start.1
  243.7 4.2 fusion
  247.9 0.0 reduce-scatter.2.cloned.1.call-update
  248.0 0.3 fusion.3
  248.2 171.3 %all-reduce.4.cloned.1.call-done = (f32[256,512]{0,1:T(8,128)}, f32[256,512]{0,1:T(8,128)}) async-done(((f32[256,512]{0,1:T(8,128)}, f32[256,512]{0,1:T(8,128)}), (f32[256,512]{0,1:T(8,128)}, f32[256,512]{0,1:T(8,128)})) %all-reduce.4.cloned.1.call-update) | async-done | bytes 1048592 | tf_op jit(solution)/shard_map/psum | solution.py:75
  419.5 1.3 broadcast_multiply_fusion
  420.8 1.0 copy.14
  421.8 1.0 copy.13
  422.8 88.9 %reduce-scatter.2.cloned.1.call-done = f32[256,256]{1,0:T(8,128)} async-done(((f32[2048,256]{1,0:T(8,128)}), f32[256,256]{1,0:T(8,128)}) %reduce-scatter.2.cloned.1.call-update) | async-done | bytes 262160 | tf_op jit(solution)/shard_map/reduce_scatter | solution.py:99
  511.8 1.7 add.67
  (14 shorter events, 0.1 us)
Async XLA Ops:
  7.2 49.9 %copy-start = (bf16[256,512]{1,0:T(8,128)(2,1)S(1)}, bf16[256,512]{1,0:T(8,128)(2,1)}, u32[]{:S(2)}) copy-start(bf16[256,512]{1,0:T(8,128)(2,1)} %param.15) | copy-start | bytes 786436
  7.2 4.9 copy-start.7
  7.2 5.1 copy-start.8
  7.2 49.8 %all-gather.2.cloned.1.call-start = ((), (), s32[]{:S(2)}) async-start(), calls=%async_computation.1 | async-start | bytes 3145728 | tf_op jit(solution)/shard_map/all_gather | solution.py:68
  7.2 24.4 %collective-permute-start.2 = (bf16[2048,256]{1,0:T(8,128)(2,1)}, bf16[2048,256]{1,0:T(8,128)(2,1)S(1)}, u32[]{:S(2)}, u32[]{:S(2)}) collective-permute-start(bf16[2048,256]{1,0:T(8,128)(2,1)} %param.8), channel_id=1, source_target_pairs={{0,16},{16,32},{32,48},{48,64},{64,80},{80,96},{96,112},{112,128},... | collective-permute-start | bytes 3145736 | tf_op jit(solution)/shard_map/ppermute | solution.py:13
  9.0 24.5 %collective-permute-start.3 = (bf16[2048,256]{1,0:T(8,128)(2,1)}, bf16[2048,256]{1,0:T(8,128)(2,1)}, u32[]{:S(2)}, u32[]{:S(2)}) collective-permute-start(bf16[2048,256]{1,0:T(8,128)(2,1)} %param.8), channel_id=1, source_target_pairs={{16,0},{32,16},{48,32},{64,48},{80,64},{96,80},{112,96},{128,112},... | collective-permute-start | bytes 3145736 | tf_op jit(solution)/shard_map/ppermute | solution.py:16
  12.0 407.5 %all-reduce.4.cloned.1.call-start = ((), (), s32[]{:S(2)}) async-start(), calls=%async_computation.3 | async-start | bytes 2097152 | tf_op jit(solution)/shard_map/psum | solution.py:75
  12.4 21.0 %copy-start.3 = (bf16[2048,256]{1,0:T(8,128)(2,1)S(1)}, bf16[2048,256]{1,0:T(8,128)(2,1)}, u32[]{:S(2)}) copy-start(bf16[2048,256]{1,0:T(8,128)(2,1)} %param.8) | copy-start | bytes 3145732
  31.7 1.0 copy-start.5
  155.9 83.2 %copy-start.2 = (bf16[2048,512]{1,0:T(8,128)(2,1)S(1)}, bf16[2048,512]{1,0:T(8,128)(2,1)}, u32[]{:S(2)}) copy-start(bf16[2048,512]{1,0:T(8,128)(2,1)} %all-gather.2.cloned.1.call-done) | copy-start | bytes 6291460
  155.9 83.2 %copy-start.4 = (bf16[2048,256]{1,0:T(8,128)(2,1)S(1)}, bf16[2048,256]{1,0:T(8,128)(2,1)}, u32[]{:S(2)}) copy-start(bf16[2048,256]{1,0:T(8,128)(2,1)} %param.8) | copy-start | bytes 3145732
  160.8 82.9 %collective-permute-start.1 = (bf16[2048,256]{1,0:T(8,128)(2,1)}, bf16[2048,256]{1,0:T(8,128)(2,1)}, u32[]{:S(2)}, u32[]{:S(2)}) collective-permute-start(bf16[2048,256]{1,0:T(8,128)(2,1)} %bitcast.6), channel_id=1, source_target_pairs={{0,16},{16,32},{32,48},{48,64},{64,80},{80,96},{96,112},{112,128},... | collective-permute-start | bytes 3145736 | tf_op jit(solution)/shard_map/ppermute | solution.py:23
  163.6 80.0 %collective-permute-start = (f32[2048,256]{1,0:T(8,128)}, f32[2048,256]{1,0:T(8,128)}, u32[]{:S(2)}, u32[]{:S(2)}) collective-permute-start(f32[2048,256]{1,0:T(8,128)} %bitcast.5), channel_id=1, source_target_pairs={{0,240},{16,0},{32,16},{48,32},{64,48},{80,64},{96,80},{112,96},{1... | collective-permute-start | bytes 6291464 | tf_op jit(solution)/shard_map/ppermute | solution.py:23
  243.6 268.1 %reduce-scatter.2.cloned.1.call-start = ((), (), s32[]{:S(2)}) async-start(), calls=%async_computation.2 | async-start | bytes 2359296 | tf_op jit(solution)/shard_map/reduce_scatter | solution.py:99
  243.7 4.3 copy-start.6
  243.7 269.7 %copy-start.1 = (bf16[256,512]{1,0:T(8,128)(2,1)S(1)}, bf16[256,512]{1,0:T(8,128)(2,1)}, u32[]{:S(2)}) copy-start(bf16[256,512]{1,0:T(8,128)(2,1)} %param.15) | copy-start | bytes 786436
Sparse Core Ops, SparseCore 0:
  12.2 20.3 all-gather.1
  243.7 175.7 all-reduce.3
  424.1 87.6 reduce-scatter.1
where the time goes:
time: 522 us; the launch traced here: 520 us
  waiting for transfers between devices  273 us (52%)
  other arithmetic  94.6 us (18%)
  blocking collectives  74.4 us (14%)
  matrix products  34.4 us (7%)
  local copies, waits for them, and re-layouts  23.9 us (5%)
  between operations  13.9 us (3%)
  starting transfers between devices  5.84 us (1%)
    psum x1, waiting for transfers between devices, local(): self_sum, neighbor_sum = lax.psum((weight_terms[0], weight_terms[1]), 'row')  171 us
    reduce_scatter x1, waiting for transfers between devices, local(): returned = lax.psum_scatter(summed, 'rep', scatter_dimension=0, tiled=True)  88.9 us
    scatter-add x1, other arithmetic, local(): jax.ops.segment_sum(contributions, positions, num_segments=3 * local_blocks)  75.1 us
    psum x1, blocking collectives, local(): aggregate = lax.psum(partial_sums, 'rep').astype(jnp.bfloat16)  74.4 us
    dot_general x1, matrix products, local(): jnp.einsum('bkij,bid->bkjd', masked_vals, neighbor_term.reshape(local_blo...  15.3 us
    dot_general x1, matrix products, local(): jnp.einsum('sij,sjd->sid', masked_vals.reshape(slot_count, block_size, bl...  12 us
    ppermute x1, waiting for transfers between devices, extended_2(): lax.ppermute(lax.slice_in_dim(block, block.shape[dim] - width, None, axis...  11.9 us
  transfers between devices with their start and end apart: 7, of which 4 were waited for; matrix products, arithmetic and copies ran while one was open for 9% of the time, Pallas kernels for 0%

commit v1 on v0

v1 whole, which is shorter than its diff:
```python
import jax
import jax.numpy as jnp
from jax import lax
from jax.experimental import pallas as pl
from jax.experimental.pallas import tpu as pltpu
from jax.sharding import PartitionSpec as P

BF = jnp.bfloat16
F32 = jnp.float32
VMEM_LIMIT = 48 * 2**20


def shifted(array, axis, by):
    size = lax.axis_size(axis)
    return lax.ppermute(array, axis, [(i, (i + by) % size) for i in range(size)])


def sparse_kernel(
    pos_ref, w_hbm, g_hbm, m_hbm, gout_ref, low_ref, own_ref, up_ref,
    acc_ref, w_ref, g_ref, m_ref, wsem, gsem, msem,
):
    blocks, slots, size, _ = w_hbm.shape
    chunks = gsem.shape[0]
    per = blocks // chunks
    rows = per * size

    def gcopy(i):
        part = pl.ds(i * rows, rows)
        return pltpu.make_async_copy(g_hbm.at[part], g_ref.at[part], gsem.at[i])

    def mcopy(i):
        part = pl.ds(i * rows, rows)
        return pltpu.make_async_copy(m_hbm.at[part], m_ref.at[part], msem.at[i])

    def wcopy(b):
        return pltpu.make_async_copy(w_hbm.at[b], w_ref.at[b], wsem.at[b])

    for i in range(chunks):
        gcopy(i).start()
        mcopy(i).start()
        for b in range(i * per, (i + 1) * per):
            wcopy(b).start()
    acc_ref[...] = jnp.zeros_like(acc_ref)

    @pl.loop(0, blocks)
    def _(b):
        @pl.when(lax.rem(b, per) == 0)
        def _():
            i = lax.div(b, per)
            gcopy(i).wait()
            mcopy(i).wait()

        wcopy(b).wait()
        part = pl.ds(pl.multiple_of(b * size, size), size)
        grad = g_ref[part, :] * m_ref[part, :].astype(BF)
        gout_ref[part, :] = grad
        grad_t = grad.T
        for s in range(0, slots, 2):
            pair = jnp.concatenate([w_ref[b, s], w_ref[b, s + 1]], axis=1)
            terms = jnp.dot(grad_t, pair, preferred_element_type=F32)
            acc_ref[pos_ref[b * slots + s]] += terms[:, :size]
            acc_ref[pos_ref[b * slots + s + 1]] += terms[:, size:]

    low_ref[...] = acc_ref[0:blocks].astype(BF)
    own_ref[...] = acc_ref[blocks : 2 * blocks]
    up_ref[...] = acc_ref[2 * blocks : 3 * blocks].astype(BF)


def sparse_pass(destinations, weights, grad, mask):
    blocks, slots, size, _ = weights.shape
    rows, width = grad.shape
    chunks = 4
    vmem = pl.BlockSpec(memory_space=pltpu.VMEM)
    hbm = pl.BlockSpec(memory_space=pltpu.HBM)
    smem = pl.BlockSpec(memory_space=pltpu.SMEM)
    side = (blocks, width, size)
    return pl.pallas_call(
        sparse_kernel,
        in_specs=[smem, hbm, hbm, hbm],
        out_specs=[vmem] * 4,
        out_shape=[
            jax.ShapeDtypeStruct((rows, width), BF),
            jax.ShapeDtypeStruct(side, BF),
            jax.ShapeDtypeStruct(side, F32),
            jax.ShapeDtypeStruct(side, BF),
        ],
        scratch_shapes=[
            pltpu.VMEM((3 * blocks + 1, width, size), F32),
            pltpu.VMEM(weights.shape, BF),
            pltpu.VMEM((rows, width), BF),
            pltpu.VMEM((rows, width), jnp.int32),
            pltpu.SemaphoreType.DMA((blocks,)),
            pltpu.SemaphoreType.DMA((chunks,)),
            pltpu.SemaphoreType.DMA((chunks,)),
        ],
        compiler_params=pltpu.CompilerParams(vmem_limit_bytes=VMEM_LIMIT),
        cost_estimate=pl.CostEstimate(
            flops=2 * blocks * slots * size * size * width,
            bytes_accessed=16 * 2**20,
            transcendentals=0,
        ),
    )(destinations, weights, grad, mask)


def pack_kernel(feat_ref, own_ref, up_ref, low_ref, fown_ref, foth_ref, out_ref, hi_ref, lo_ref):
    blocks, width, size = own_ref.shape
    parts = out_ref.shape[0]
    per = blocks // parts
    for b in range(blocks):
        total = own_ref[b] + up_ref[b].astype(F32) + low_ref[b].astype(F32)
        hi = total.astype(BF)
        out_ref[b // per, (b % per) * width : (b % per + 1) * width, :] = hi
        hi_ref[:, b * size : (b + 1) * size] = hi
        lo_ref[:, b * size : (b + 1) * size] = (total - hi.astype(F32)).astype(BF)
    products = []
    for f_ref in (fown_ref, foth_ref):
        products.append(
            jnp.dot(hi_ref[...], f_ref[...], preferred_element_type=F32)
            + jnp.dot(lo_ref[...], f_ref[...], preferred_element_type=F32)
        )
    first = feat_ref[0] == 0
    rows = width // parts
    base = per * width
    for f in range(2):
        value = jnp.where(first, products[f], products[1 - f])
        hi = value.astype(BF)
        lo = (value - hi.astype(F32)).astype(BF)
        for level, piece in enumerate((hi, lo)):
            for c in range(width // size):
                at = base + ((f * 2 + level) * (width // size) + c) * rows
                for p in range(parts):
                    out_ref[p, at : at + rows, :] = piece[
                        p * rows : (p + 1) * rows, c * size : (c + 1) * size
                    ]


def pack(feat_index, own, up, low, features, features_other, parts):
    blocks, width, size = own.shape
    vmem = pl.BlockSpec(memory_space=pltpu.VMEM)
    smem = pl.BlockSpec(memory_space=pltpu.SMEM)
    rows = (blocks // parts) * width + 4 * (width // size) * (width // parts)
    return pl.pallas_call(
        pack_kernel,
        in_specs=[smem] + [vmem] * 5,
        out_specs=vmem,
        out_shape=jax.ShapeDtypeStruct((parts, rows, size), BF),
        scratch_shapes=[
            pltpu.VMEM((width, blocks * size), BF),
            pltpu.VMEM((width, blocks * size), BF),
        ],
        compiler_params=pltpu.CompilerParams(vmem_limit_bytes=VMEM_LIMIT),
    )(feat_index, own, up, low, features, features_other)


def finish_kernel(own_ref, oth_ref, wown_ref, woth_ref, self_ref, out_ref):
    per, width, size = own_ref.shape
    for b in range(per):
        total = self_ref[b * size : (b + 1) * size, :]
        for h_ref, w_ref in ((own_ref, wown_ref), (oth_ref, woth_ref)):
            h = h_ref[b].T
            hi = h.astype(BF)
            lo = (h - hi.astype(F32)).astype(BF)
            for piece in (hi, lo):
                total += lax.dot_general(
                    piece, w_ref[...], (((1,), (1,)), ((), ())), preferred_element_type=F32
                )
        out_ref[b * size : (b + 1) * size, :] = total


def finish(h_own, h_other, w_own, w_other, self_term):
    vmem = pl.BlockSpec(memory_space=pltpu.VMEM)
    return pl.pallas_call(
        finish_kernel,
        in_specs=[vmem] * 5,
        out_specs=vmem,
        out_shape=jax.ShapeDtypeStruct(self_term.shape, F32),
        compiler_params=pltpu.CompilerParams(vmem_limit_bytes=VMEM_LIMIT),
    )(h_own, h_other, w_own, w_other, self_term)


def row_sum(piece):
    count = lax.axis_size("row")
    sent = jnp.broadcast_to(piece.astype(BF)[None], (count,) + piece.shape)
    return lax.all_to_all(sent, "row", 0, 0).astype(F32).sum(0)


def collect(piece, scaling):
    reps, feats = lax.axis_size("rep"), lax.axis_size("feat")
    halves, columns, rows, lanes = piece.shape
    sent = jnp.broadcast_to((piece * scaling)[:, None], (halves, reps, columns, rows, lanes))
    sent = sent.reshape(feats * reps, columns, rows, lanes)
    got = lax.all_to_all(sent, ("feat", "rep"), 0, 0)
    return got.transpose(1, 3, 0, 2).reshape(columns * lanes, feats * reps * rows)


def local(
    features,
    grad_out,
    relu_mask,
    block_columns,
    block_count,
    block_weights,
    self_weight,
    neighbor_weight,
):
    row_devices = lax.axis_size("row")
    rep_devices = lax.axis_size("rep")
    row_index = lax.axis_index("row")
    rep_index = lax.axis_index("rep")
    feat_index = lax.axis_index("feat")
    first = feat_index == 0
    local_blocks, slot_width = block_columns.shape
    block_size = block_weights.shape[2]
    row_count, half_width = features.shape
    share_rows = row_count // rep_devices
    share_start = rep_index * share_rows
    scaling = float(row_count * row_devices) ** (-0.5)

    slot_number = rep_index * slot_width + jnp.arange(slot_width, dtype=jnp.int32)
    live_slots = slot_number[None, :] < block_count[:, None]
    relative = (block_columns // local_blocks - row_index) % row_devices
    side = jnp.where(relative == row_devices - 1, 0, jnp.where(relative == 0, 1, 2))
    destinations = jnp.where(
        live_slots, side * local_blocks + block_columns % local_blocks, 3 * local_blocks
    ).reshape(-1)

    features_other = shifted(features, "feat", 1)
    masked_grad, to_lower, own, to_upper = sparse_pass(
        destinations, block_weights, grad_out, relu_mask
    )
    from_upper = shifted(to_lower, "row", -1)
    from_lower = shifted(to_upper, "row", 1)

    lanes = block_size
    chunks = half_width // lanes
    share = half_width // rep_devices

    def self_part(values):
        whole = jnp.einsum("ro,rd->od", masked_grad, values, preferred_element_type=F32)
        mine = lax.dynamic_slice_in_dim(whole, rep_index * share, share, 0)
        return mine.reshape(share, chunks, lanes).transpose(1, 0, 2)

    self_own = self_part(features)
    self_oth = self_part(features_other)
    self_piece = jnp.stack(
        [jnp.where(first, self_own, self_oth), jnp.where(first, self_oth, self_own)]
    )
    self_grad = collect(row_sum(self_piece), scaling)

    grad_rows = lax.dynamic_slice_in_dim(masked_grad, share_start, share_rows, 0)
    grad_rows_other = shifted(grad_rows, "feat", 1)

    def halves(weight):
        left, right = weight[:, :half_width], weight[:, half_width:]
        return jnp.where(first, left, right), jnp.where(first, right, left)

    self_w_own, self_w_oth = halves(self_weight)
    neighbor_w_own, neighbor_w_oth = halves(neighbor_weight)
    self_term = jnp.einsum(
        "ro,do->rd", grad_rows, self_w_own, preferred_element_type=F32
    ) + jnp.einsum("ro,do->rd", grad_rows_other, self_w_oth, preferred_element_type=F32)

    payload = pack(
        feat_index.reshape(1).astype(jnp.int32),
        own, from_upper, from_lower, features, features_other, rep_devices,
    )
    got = lax.all_to_all(payload, "rep", 0, 0).astype(F32).sum(0)
    share_blocks = local_blocks // rep_devices
    edge = share_blocks * half_width
    h_own = got[:edge].reshape(share_blocks, half_width, lanes)
    h_other = shifted(h_own, "feat", 1)
    features_grad = finish(h_own, h_other, neighbor_w_own, neighbor_w_oth, self_term)

    neighbor_piece = got[edge:].reshape(2, 2, chunks, share, lanes).sum(1)
    neighbor_grad = collect(row_sum(neighbor_piece), scaling)
    return (features_grad, self_grad, neighbor_grad)


def solution(mesh):
    return jax.shard_map(
        local,
        mesh=mesh,
        in_specs=(
            P("row", "feat"),
            P("row", "feat"),
            P("row", "feat"),
            P("row", "rep"),
            P("row"),
            P("row", "rep", None, None),
            P("feat", None),
            P("feat", None),
        ),
        out_specs=(P(("row", "rep"), "feat"), P("feat", None), P("feat", None)),
        check_vma=False,
    )
```

time: 522 us -> 161 us (0.31)
  waiting for transfers between devices: 273 us -> 93.5 us
  other arithmetic: 94.6 us -> 2.7 us
  blocking collectives: 74.4 us -> 0 us
  matrix products: 34.4 us -> 1.41 us
  starting transfers between devices: 5.84 us -> 35 us
  Pallas kernels: 0 us -> 18.7 us
  local copies, waits for them, and re-layouts: 23.9 us -> 7.38 us
  between operations: 13.9 us -> 0.83 us
    psum x1 -> x0, waiting for transfers between devices: 171 us -> none  [local(): self_sum, neighbor_sum = lax.psum((weight_terms[0], weight_terms[1]), 'row')]
    reduce_scatter x1 -> x0, waiting for transfers between devices: 88.9 us -> none  [local(): returned = lax.psum_scatter(summed, 'rep', scatter_dimension=0, tiled=True)]
    scatter-add x1 -> x0, other arithmetic: 75.1 us -> none  [local(): jax.ops.segment_sum(contributions, positions, num_segments=3 * local_blocks)]
    psum x1 -> x0, blocking collectives: 74.4 us -> none  [local(): aggregate = lax.psum(partial_sums, 'rep').astype(jnp.bfloat16)]
    all_to_all x0 -> x5, waiting for transfers between devices: none -> 65.2 us  [the longest x2 25.4 us: row_sum(): return lax.all_to_all(sent, 'row', 0, 0).astype(F32).sum(0)]
    dot_general x6 -> x4, matrix products: 34.4 us -> 1.41 us  [the longest x2 0.96 us: self_part(): jnp.einsum('ro,rd->od', masked_grad, values, preferred_element_type=F32)]
    all_to_all x0 -> x5, starting transfers between devices: none -> 32 us  [the longest x2 13.9 us: collect(): got = lax.all_to_all(sent, ('feat', 'rep'), 0, 0)]
    ppermute x2 -> x5, waiting for transfers between devices: 0.01 us -> 28.3 us  [shifted(): lax.ppermute(array, axis, [(i, (i + by) % size) for i in range(size)])]
  transfers between devices with their start and end apart: 7 -> 10, of which waited for: 4 -> 7; matrix products, arithmetic and copies ran while one was open for 9% -> 4% of each run, Pallas kernels for 0% -> 9%
where the time goes in v1:
time: 161 us; the launch traced here: 160 us
  waiting for transfers between devices  93.5 us (58%)
  starting transfers between devices  35 us (22%)
  Pallas kernels  18.7 us (12%)
  local copies, waits for them, and re-layouts  7.38 us (5%)
  other arithmetic  2.7 us (2%)
    ppermute x5, waiting for transfers between devices, shifted(): lax.ppermute(array, axis, [(i, (i + by) % size) for i in range(size)])  28.3 us
    all_to_all x2, waiting for transfers between devices, row_sum(): return lax.all_to_all(sent, 'row', 0, 0).astype(F32).sum(0)  25.4 us
    all_to_all x2, waiting for transfers between devices, collect(): got = lax.all_to_all(sent, ('feat', 'rep'), 0, 0)  20.7 us
    all_to_all x1, waiting for transfers between devices, local(): got = lax.all_to_all(payload, 'rep', 0, 0).astype(F32).sum(0)  19.2 us
    all_to_all x2, starting transfers between devices, collect(): got = lax.all_to_all(sent, ('feat', 'rep'), 0, 0)  13.9 us
    pallas_call x1, Pallas kernels, sparse_pass(): pl.pallas_call(sparse_kernel, in_specs=[smem, hbm, hbm, hbm], out_specs=[...  12.7 us
    all_to_all x2, starting transfers between devices, row_sum(): return lax.all_to_all(sent, 'row', 0, 0).astype(F32).sum(0)  11.7 us
    all_to_all x1, starting transfers between devices, local(): got = lax.all_to_all(payload, 'rep', 0, 0).astype(F32).sum(0)  6.34 us
  transfers between devices with their start and end apart: 10, of which 7 were waited for; matrix products, arithmetic and copies ran while one was open for 4% of the time, Pallas kernels for 9%

profile of v1, /device:TPU:33, one launch (start us, length us, event | category | flops | bytes accessed | tf_op | source)
XLA Modules:
  0.0 159.5 jit_solution(10422795272604114134)
XLA Ops:
  0.6 0.8 collective-permute-start.2
  1.4 0.8 fusion.12
  2.2 0.1 reshape.72.pos_ref
  2.2 0.0 copy-start.1
  2.2 1.2 copy-done.1
  3.5 0.0 copy-start
  3.5 12.7 %shard_map.103 = (bf16[2048,256]{1,0:T(8,128)(2,1)S(1)}, bf16[16,256,128]{2,1,0:T(8,128)(2,1)}, f32[16,256,128]{2,1,0:T(8,128)}, bf16[16,256,128]{2,1,0:T(8,128)(2,1)}) custom-call(s32[256]{0:T(256)S(1)} %reshape.72.pos_ref, bf16[16,16,128,128]{3,2,1,0:T(8,128)(2,1)} %w_hbm.1, bf16[2048,256]{1,0:T(8,128)(2,1)S(1)} %copy-done.1, s32[2048,256]{1,0:T(8,128)} %m_hbm.1), custom_call_target="tpu_custom_call" | custom-call | flops 2147483648 | bytes 16777216 | tf_op jit(solution)/shard_map/pallas_call | solution.py:77
  16.2 1.6 %collective-permute-start = (bf16[16,256,128]{2,1,0:T(8,128)(2,1)}, bf16[16,256,128]{2,1,0:T(8,128)(2,1)}, u32[]{:S(2)}, u32[]{:S(2)}) collective-permute-start(bf16[16,256,128]{2,1,0:T(8,128)(2,1)} %get-tuple-element.8), channel_id=1, source_target_pairs={{0,240},{16,0},{32,16},{48,32},{64,48},{80,64},{96,80},{112,96},{1... | collective-permute-start | bytes 3145736 | tf_op jit(solution)/shard_map/ppermute | solution.py:15
  17.8 0.2 collective-permute-start.1
  18.0 0.0 collective-permute-done.2.foth_ref
  18.0 23.6 %collective-permute-done.up_ref = bf16[16,256,128]{2,1,0:T(8,128)(2,1)} collective-permute-done((bf16[16,256,128]{2,1,0:T(8,128)(2,1)}, bf16[16,256,128]{2,1,0:T(8,128)(2,1)}, u32[]{:S(2)}, u32[]{:S(2)}) %collective-permute-start) | collective-permute-done | bytes 1048608 | tf_op jit(solution)/shard_map/ppermute | solution.py:15
  41.6 4.6 %collective-permute-done.1.low_ref = bf16[16,256,128]{2,1,0:T(8,128)(2,1)} collective-permute-done((bf16[16,256,128]{2,1,0:T(8,128)(2,1)}, bf16[16,256,128]{2,1,0:T(8,128)(2,1)}, u32[]{:S(2)}, u32[]{:S(2)}) %collective-permute-start.1) | collective-permute-done | bytes 1048608 | tf_op jit(solution)/shard_map/ppermute | solution.py:15
  46.2 0.0 copy-done
  46.2 4.8 %shard_map.104 = bf16[8,768,128]{2,1,0:T(8,128)(2,1)} custom-call(s32[1]{0:T(128)} %bitcast.feat_ref, f32[16,256,128]{2,1,0:T(8,128)} %get-tuple-element.7.own_ref, bf16[16,256,128]{2,1,0:T(8,128)(2,1)} %collective-permute-done.up_ref, bf16[16,256,128]{2,1,0:T(8,128)(2,1)} %collective-permute-done.1.low_ref, bf16[2048,256]{1,0:T(8,128)(2,1)S(1)} %copy-done, ...), custom_call_target="tpu_custom_call" | custom-call | tf_op jit(solution)/shard_map/pallas_call | solution.py:142
  51.0 6.3 %all-to-all-start = ((bf16[8,768,128]{2,1,0:T(8,128)(2,1)}), bf16[8,768,128]{2,1,0:T(8,128)(2,1)}, u32[]{:S(2)}, u32[]{:S(2)}) async-start(bf16[8,768,128]{2,1,0:T(8,128)(2,1)} %shard_map.104), calls=%async_computation | async-start | bytes 3145728 | tf_op jit(solution)/shard_map/all_to_all | solution.py:267
  57.4 0.5 fusion.14
  57.8 0.5 fusion.15
  58.5 19.2 %all-to-all-done = bf16[8,768,128]{2,1,0:T(8,128)(2,1)} async-done(((bf16[8,768,128]{2,1,0:T(8,128)(2,1)}), bf16[8,768,128]{2,1,0:T(8,128)(2,1)}, u32[]{:S(2)}, u32[]{:S(2)}) %all-to-all-start) | async-done | bytes 1572896 | tf_op jit(solution)/shard_map/all_to_all | solution.py:267
  77.7 0.9 broadcast_in_dim.22
  78.6 6.3 %all-to-all-start.1 = ((bf16[16,2,2,32,128]{4,3,2,1,0:T(8,128)(2,1)}), bf16[16,2,2,32,128]{4,3,2,1,0:T(8,128)(2,1)S(1)}, u32[]{:S(2)}, u32[]{:S(2)}) async-start(bf16[16,2,2,32,128]{4,3,2,1,0:T(8,128)(2,1)} %broadcast_in_dim.22), calls=%async_computation.1 | async-start | bytes 1048576 | tf_op jit(solution)/shard_map/all_to_all | solution.py:184
  84.9 1.7 %convert_reduce_fusion = f32[768,128]{1,0:T(8,128)S(1)} fusion(bf16[8,768,128]{2,1,0:T(8,128)(2,1)} %all-to-all-done), kind=kLoop, calls=%fused_computation | loop fusion | flops 1474560 | bytes 1966080 | tf_op jit(solution)/shard_map/reduce_sum | solution.py:267
  86.6 12.0 %all-to-all-done.1 = bf16[16,2,2,32,128]{4,3,2,1,0:T(8,128)(2,1)S(1)} async-done(((bf16[16,2,2,32,128]{4,3,2,1,0:T(8,128)(2,1)}), bf16[16,2,2,32,128]{4,3,2,1,0:T(8,128)(2,1)S(1)}, u32[]{:S(2)}, u32[]{:S(2)}) %all-to-all-start.1) | async-done | bytes 524320 | tf_op jit(solution)/shard_map/all_to_all | solution.py:184
  98.5 0.9 broadcast_in_dim.24
  99.5 5.4 %all-to-all-start.3 = ((bf16[16,2,2,32,128]{4,3,2,1,0:T(8,128)(2,1)}), bf16[16,2,2,32,128]{4,3,2,1,0:T(8,128)(2,1)S(1)}, u32[]{:S(2)}, u32[]{:S(2)}) async-start(bf16[16,2,2,32,128]{4,3,2,1,0:T(8,128)(2,1)} %broadcast_in_dim.24), calls=%async_computation.3 | async-start | bytes 1048576 | tf_op jit(solution)/shard_map/all_to_all | solution.py:184
  104.9 0.1 convert_reduce_fusion.2
  105.0 0.1 copy.16
  105.0 0.0 copy-start.3
  105.1 13.4 %all-to-all-done.3 = bf16[16,2,2,32,128]{4,3,2,1,0:T(8,128)(2,1)S(1)} async-done(((bf16[16,2,2,32,128]{4,3,2,1,0:T(8,128)(2,1)}), bf16[16,2,2,32,128]{4,3,2,1,0:T(8,128)(2,1)S(1)}, u32[]{:S(2)}, u32[]{:S(2)}) %all-to-all-start.3) | async-done | bytes 524320 | tf_op jit(solution)/shard_map/all_to_all | solution.py:184
  118.5 1.0 broadcast_in_dim.23
  119.5 10.3 %all-to-all-start.2 = ((f32[16,2,32,128]{3,1,2,0:T(2,128)}), f32[16,2,32,128]{3,1,2,0:T(2,128)S(1)}, u32[]{:S(2)}, u32[]{:S(2)}) async-start(f32[16,2,32,128]{3,1,2,0:T(2,128)} %bitcast.6), calls=%async_computation.2 | async-start | bytes 1048576 | tf_op jit(solution)/shard_map/all_to_all | solution.py:192
  129.8 0.0 copy-start.2
  129.8 0.2 collective-permute-start.4
  130.0 0.1 convert_reduce_fusion.1
  130.1 0.1 copy.17
  130.1 11.7 %all-to-all-done.2 = f32[16,2,32,128]{3,1,2,0:T(2,128)S(1)} async-done(((f32[16,2,32,128]{3,1,2,0:T(2,128)}), f32[16,2,32,128]{3,1,2,0:T(2,128)S(1)}, u32[]{:S(2)}, u32[]{:S(2)}) %all-to-all-start.2) | async-done | bytes 524320 | tf_op jit(solution)/shard_map/all_to_all | solution.py:192
  141.8 1.0 broadcast_in_dim.25
  142.8 3.6 %all-to-all-start.4 = ((f32[16,2,32,128]{3,1,2,0:T(2,128)}), f32[16,2,32,128]{3,1,2,0:T(2,128)S(1)}, u32[]{:S(2)}, u32[]{:S(2)}) async-start(f32[16,2,32,128]{3,1,2,0:T(2,128)} %bitcast.9), calls=%async_computation.4 | async-start | bytes 1048576 | tf_op jit(solution)/shard_map/all_to_all | solution.py:192
  146.4 0.0 copy-done.3
  146.4 0.2 fusion.1
  146.7 0.3 collective-permute-start.3
  147.0 0.0 copy-done.2
  147.0 0.0 collective-permute-done.4
  147.0 0.2 convolution_add_fusion.self_ref
  147.3 1.0 copy.18
  148.3 0.0 collective-permute-done.3.oth_ref
  148.3 1.2 shard_map.105
  149.5 9.0 %all-to-all-done.4 = f32[16,2,32,128]{3,1,2,0:T(2,128)S(1)} async-done(((f32[16,2,32,128]{3,1,2,0:T(2,128)}), f32[16,2,32,128]{3,1,2,0:T(2,128)S(1)}, u32[]{:S(2)}, u32[]{:S(2)}) %all-to-all-start.4) | async-done | bytes 524320 | tf_op jit(solution)/shard_map/all_to_all | solution.py:192
  158.5 1.0 copy.19
  (15 shorter events, 0.3 us)
Async XLA Ops:
  0.6 17.3 %collective-permute-start.2 = (bf16[2048,256]{1,0:T(8,128)(2,1)}, bf16[2048,256]{1,0:T(8,128)(2,1)S(1)}, u32[]{:S(2)}, u32[]{:S(2)}) collective-permute-start(bf16[2048,256]{1,0:T(8,128)(2,1)} %fown_ref.1), channel_id=1, source_target_pairs={{0,1},{1,0},{2,3},{3,2},{4,5},{5,4},{6,7},{7,6},{8,9},{9,8},{10,11... | collective-permute-start | bytes 3145736 | tf_op jit(solution)/shard_map/ppermute | solution.py:15
  2.2 1.2 copy-start.1
  3.5 42.7 %copy-start = (bf16[2048,256]{1,0:T(8,128)(2,1)S(1)}, bf16[2048,256]{1,0:T(8,128)(2,1)}, u32[]{:S(2)}) copy-start(bf16[2048,256]{1,0:T(8,128)(2,1)} %fown_ref.1) | copy-start | bytes 3145732
  16.2 25.4 %collective-permute-start = (bf16[16,256,128]{2,1,0:T(8,128)(2,1)}, bf16[16,256,128]{2,1,0:T(8,128)(2,1)}, u32[]{:S(2)}, u32[]{:S(2)}) collective-permute-start(bf16[16,256,128]{2,1,0:T(8,128)(2,1)} %get-tuple-element.8), channel_id=1, source_target_pairs={{0,240},{16,0},{32,16},{48,32},{64,48},{80,64},{96,80},{112,96},{1... | collective-permute-start | bytes 3145736 | tf_op jit(solution)/shard_map/ppermute | solution.py:15
  17.8 28.4 %collective-permute-start.1 = (bf16[16,256,128]{2,1,0:T(8,128)(2,1)}, bf16[16,256,128]{2,1,0:T(8,128)(2,1)}, u32[]{:S(2)}, u32[]{:S(2)}) collective-permute-start(bf16[16,256,128]{2,1,0:T(8,128)(2,1)} %get-tuple-element.9), channel_id=1, source_target_pairs={{0,16},{16,32},{32,48},{48,64},{64,80},{80,96},{96,112},{112,128},... | collective-permute-start | bytes 3145736 | tf_op jit(solution)/shard_map/ppermute | solution.py:15
  51.0 26.6 %all-to-all-start = ((bf16[8,768,128]{2,1,0:T(8,128)(2,1)}), bf16[8,768,128]{2,1,0:T(8,128)(2,1)}, u32[]{:S(2)}, u32[]{:S(2)}) async-start(bf16[8,768,128]{2,1,0:T(8,128)(2,1)} %shard_map.104), calls=%async_computation | async-start | bytes 3145728 | tf_op jit(solution)/shard_map/all_to_all | solution.py:267
  78.6 20.0 %all-to-all-start.1 = ((bf16[16,2,2,32,128]{4,3,2,1,0:T(8,128)(2,1)}), bf16[16,2,2,32,128]{4,3,2,1,0:T(8,128)(2,1)S(1)}, u32[]{:S(2)}, u32[]{:S(2)}) async-start(bf16[16,2,2,32,128]{4,3,2,1,0:T(8,128)(2,1)} %broadcast_in_dim.22), calls=%async_computation.1 | async-start | bytes 1048576 | tf_op jit(solution)/shard_map/all_to_all | solution.py:184
  99.5 19.0 %all-to-all-start.3 = ((bf16[16,2,2,32,128]{4,3,2,1,0:T(8,128)(2,1)}), bf16[16,2,2,32,128]{4,3,2,1,0:T(8,128)(2,1)S(1)}, u32[]{:S(2)}, u32[]{:S(2)}) async-start(bf16[16,2,2,32,128]{4,3,2,1,0:T(8,128)(2,1)} %broadcast_in_dim.24), calls=%async_computation.3 | async-start | bytes 1048576 | tf_op jit(solution)/shard_map/all_to_all | solution.py:184
  105.0 41.4 %copy-start.3 = (bf16[256,512]{1,0:T(8,128)(2,1)S(1)}, bf16[256,512]{1,0:T(8,128)(2,1)}, u32[]{:S(2)}) copy-start(bf16[256,512]{1,0:T(8,128)(2,1)} %param.14) | copy-start | bytes 786436
  119.5 22.4 %all-to-all-start.2 = ((f32[16,2,32,128]{3,1,2,0:T(2,128)}), f32[16,2,32,128]{3,1,2,0:T(2,128)S(1)}, u32[]{:S(2)}, u32[]{:S(2)}) async-start(f32[16,2,32,128]{3,1,2,0:T(2,128)} %bitcast.6), calls=%async_computation.2 | async-start | bytes 1048576 | tf_op jit(solution)/shard_map/all_to_all | solution.py:192
  129.8 17.2 %copy-start.2 = (bf16[256,512]{1,0:T(8,128)(2,1)S(1)}, bf16[256,512]{1,0:T(8,128)(2,1)}, u32[]{:S(2)}) copy-start(bf16[256,512]{1,0:T(8,128)(2,1)} %param.15) | copy-start | bytes 786436
  129.8 17.2 %collective-permute-start.4 = (bf16[256,256]{1,0:T(8,128)(2,1)S(1)}, bf16[256,256]{1,0:T(8,128)(2,1)S(1)}, u32[]{:S(2)}, u32[]{:S(2)}) collective-permute-start(bf16[256,256]{1,0:T(8,128)(2,1)S(1)} %constant_dynamic-slice_fusion), channel_id=1, source_target_pairs={{0,1},{1,0},{2,3},{3,2},{4,5},{5,4},{6,7},{7,6},{8,9},{9,8},{10,11... | collective-permute-start | bytes 393224 | tf_op jit(solution)/shard_map/ppermute | solution.py:15
  142.8 15.7 %all-to-all-start.4 = ((f32[16,2,32,128]{3,1,2,0:T(2,128)}), f32[16,2,32,128]{3,1,2,0:T(2,128)S(1)}, u32[]{:S(2)}, u32[]{:S(2)}) async-start(f32[16,2,32,128]{3,1,2,0:T(2,128)} %bitcast.9), calls=%async_computation.4 | async-start | bytes 1048576 | tf_op jit(solution)/shard_map/all_to_all | solution.py:192
  146.7 1.6 %collective-permute-start.3 = (f32[2,256,128]{2,1,0:T(8,128)S(1)}, f32[2,256,128]{2,1,0:T(8,128)S(1)}, u32[]{:S(2)}, u32[]{:S(2)}) collective-permute-start(f32[2,256,128]{2,1,0:T(8,128)S(1)} %bitcast.33), channel_id=1, source_target_pairs={{0,1},{1,0},{2,3},{3,2},{4,5},{5,4},{6,7},{7,6},{8,9},{9,8},{10,11... | collective-permute-start | bytes 786440 | tf_op jit(solution)/shard_map/ppermute | solution.py:15

commit v2 on v1

v2 whole, which is shorter than its diff:
```python
import jax
import jax.numpy as jnp
from jax import lax
from jax.experimental import pallas as pl
from jax.experimental.pallas import tpu as pltpu
from jax.sharding import PartitionSpec as P

BF = jnp.bfloat16
F32 = jnp.float32
VMEM_LIMIT = 48 * 2**20


def shifted(array, axis, by):
    size = lax.axis_size(axis)
    return lax.ppermute(array, axis, [(i, (i + by) % size) for i in range(size)])


def sparse_kernel(
    pos_ref, w_hbm, g_ref, out_ref, acc_ref, w_ref, wsem
):
    blocks, slots, size, _ = w_hbm.shape

    def wcopy(b):
        return pltpu.make_async_copy(w_hbm.at[b], w_ref.at[b], wsem.at[b])

    for b in range(blocks):
        wcopy(b).start()
    acc_ref[...] = jnp.zeros_like(acc_ref)

    @pl.loop(0, blocks)
    def _(b):
        wcopy(b).wait()
        part = pl.ds(pl.multiple_of(b * size, size), size)
        grad_t = g_ref[part, :].T
        for s in range(0, slots, 2):
            pair = jnp.concatenate([w_ref[b, s], w_ref[b, s + 1]], axis=1)
            terms = jnp.dot(grad_t, pair, preferred_element_type=F32)
            acc_ref[pos_ref[b * slots + s]] += terms[:, :size]
            acc_ref[pos_ref[b * slots + s + 1]] += terms[:, size:]

    width = g_ref.shape[1]
    pieces = blocks // out_ref.shape[0]
    for side in range(3):
        for b in range(blocks):
            at = (side * pieces + b % pieces) * width
            out_ref[b // pieces, at : at + width, :] = acc_ref[side * blocks + b].astype(BF)


def sparse_pass(destinations, weights, grad, parts):
    blocks, slots, size, _ = weights.shape
    width = grad.shape[1]
    vmem = pl.BlockSpec(memory_space=pltpu.VMEM)
    hbm = pl.BlockSpec(memory_space=pltpu.HBM)
    smem = pl.BlockSpec(memory_space=pltpu.SMEM)
    pieces = blocks // parts
    return pl.pallas_call(
        sparse_kernel,
        in_specs=[smem, hbm, vmem],
        out_specs=vmem,
        out_shape=jax.ShapeDtypeStruct((parts, 3 * pieces * width, size), BF),
        scratch_shapes=[
            pltpu.VMEM((3 * blocks + 1, width, size), F32),
            pltpu.VMEM(weights.shape, BF),
            pltpu.SemaphoreType.DMA((blocks,)),
        ],
        compiler_params=pltpu.CompilerParams(vmem_limit_bytes=VMEM_LIMIT),
        cost_estimate=pl.CostEstimate(
            flops=2 * blocks * slots * size * size * width,
            bytes_accessed=13 * 2**20,
            transcendentals=0,
        ),
    )(destinations, weights, grad)


def product_kernel(feat_ref, sums_ref, *refs):
    f_refs, out_ref, h_ref = refs[:6], refs[6], refs[7]
    parts, depth, size = sums_ref.shape
    width = f_refs[0].shape[1]
    pieces = depth // (3 * width)
    for side in range(3):
        for b in range(parts * pieces):
            at = (side * pieces + b % pieces) * width
            h_ref[side, :, b * size : (b + 1) * size] = sums_ref[b // pieces, at : at + width, :]
    products = []
    for which in range(2):
        total = jnp.zeros((width, width), F32)
        for side in range(3):
            total += jnp.dot(
                h_ref[side], f_refs[side * 2 + which][...], preferred_element_type=F32
            )
        products.append(total)
    first = feat_ref[0] == 0
    targets = out_ref.shape[0]
    rows = width // targets
    chunks = width // size
    for f in range(2):
        piece = jnp.where(first, products[f], products[1 - f]).astype(BF)
        for c in range(chunks):
            at = (f * chunks + c) * rows
            for t in range(targets):
                out_ref[t, at : at + rows, :] = piece[
                    t * rows : (t + 1) * rows, c * size : (c + 1) * size
                ]


def product(feat_index, sums, features, targets):
    size = sums.shape[2]
    rows, width = features[0].shape
    vmem = pl.BlockSpec(memory_space=pltpu.VMEM)
    smem = pl.BlockSpec(memory_space=pltpu.SMEM)
    depth = 2 * (width // size) * (width // targets)
    return pl.pallas_call(
        product_kernel,
        in_specs=[smem] + [vmem] * (1 + len(features)),
        out_specs=vmem,
        out_shape=jax.ShapeDtypeStruct((targets, depth, size), BF),
        scratch_shapes=[pltpu.VMEM((3, width, rows), BF)],
        compiler_params=pltpu.CompilerParams(vmem_limit_bytes=VMEM_LIMIT),
        cost_estimate=pl.CostEstimate(
            flops=90 * rows * width * width, bytes_accessed=10 * 2**20, transcendentals=0
        ),
    )(feat_index, sums, *features)


def finish_kernel(own_ref, oth_ref, wown_ref, woth_ref, self_ref, out_ref):
    per, width, size = own_ref.shape
    for b in range(per):
        total = self_ref[b * size : (b + 1) * size, :]
        for h_ref, w_ref in ((own_ref, wown_ref), (oth_ref, woth_ref)):
            h = h_ref[b].T
            hi = h.astype(BF)
            lo = (h - hi.astype(F32)).astype(BF)
            for piece in (hi, lo):
                total += lax.dot_general(
                    piece, w_ref[...], (((1,), (1,)), ((), ())), preferred_element_type=F32
                )
        out_ref[b * size : (b + 1) * size, :] = total


def finish(h_own, h_other, w_own, w_other, self_term):
    vmem = pl.BlockSpec(memory_space=pltpu.VMEM)
    return pl.pallas_call(
        finish_kernel,
        in_specs=[vmem] * 5,
        out_specs=vmem,
        out_shape=jax.ShapeDtypeStruct(self_term.shape, F32),
        compiler_params=pltpu.CompilerParams(vmem_limit_bytes=VMEM_LIMIT),
    )(h_own, h_other, w_own, w_other, self_term)


def exchanged(value, step):
    count = lax.axis_size("row")
    return value + lax.ppermute(value, "row", [(i, i ^ step) for i in range(count)])


def whole(pieces, scaling):
    count, columns, rows, lanes = pieces.shape
    scaled = pieces.astype(F32) * scaling
    return scaled.transpose(1, 3, 0, 2).reshape(columns * lanes, count * rows)


def collect(piece):
    rows, feats = lax.axis_size("row"), lax.axis_size("feat")
    sent = jnp.broadcast_to(piece[:, None], (feats, rows) + piece.shape[1:])
    sent = sent.reshape((feats * rows,) + piece.shape[1:])
    return lax.all_to_all(sent, ("feat", "row"), 0, 0)


def local(
    features,
    grad_out,
    relu_mask,
    block_columns,
    block_count,
    block_weights,
    self_weight,
    neighbor_weight,
):
    row_devices = lax.axis_size("row")
    rep_devices = lax.axis_size("rep")
    row_index = lax.axis_index("row")
    rep_index = lax.axis_index("rep")
    feat_index = lax.axis_index("feat")
    first = feat_index == 0
    local_blocks, slot_width = block_columns.shape
    block_size = block_weights.shape[2]
    row_count, half_width = features.shape
    share_rows = row_count // rep_devices
    share_start = rep_index * share_rows
    scaling = float(row_count * row_devices) ** (-0.5)

    slot_number = rep_index * slot_width + jnp.arange(slot_width, dtype=jnp.int32)
    live_slots = slot_number[None, :] < block_count[:, None]
    relative = (block_columns // local_blocks - row_index) % row_devices
    side = jnp.where(relative == row_devices - 1, 0, jnp.where(relative == 0, 1, 2))
    destinations = jnp.where(
        live_slots, side * local_blocks + block_columns % local_blocks, 3 * local_blocks
    ).reshape(-1)

    before, after = shifted(features, "row", 1), shifted(features, "row", -1)
    features_other = shifted(features, "feat", 1)
    masked_grad = grad_out * relu_mask.astype(BF)

    lanes = block_size
    chunks = half_width // lanes
    share = half_width // rep_devices

    def self_part(values):
        whole = jnp.einsum("ro,rd->od", masked_grad, values, preferred_element_type=F32)
        mine = lax.dynamic_slice_in_dim(whole, rep_index * share, share, 0)
        return mine.reshape(share, chunks, lanes).transpose(1, 0, 2)

    self_own = self_part(features)
    self_oth = self_part(features_other)
    self_piece = jnp.stack(
        [jnp.where(first, self_own, self_oth), jnp.where(first, self_oth, self_own)]
    )
    self_piece, grad_values = lax.optimization_barrier((self_piece, masked_grad))
    sums = sparse_pass(destinations, block_weights, grad_values, rep_devices)
    sums_got = lax.all_to_all(sums, "rep", 0, 0)
    before, after, sums = lax.optimization_barrier((before, after, sums))
    extended = []
    for rows, other in ((before, None), (features, features_other), (after, None)):
        extended += [rows, shifted(rows, "feat", 1) if other is None else other]

    grad_rows = lax.dynamic_slice_in_dim(masked_grad, share_start, share_rows, 0)
    grad_rows_other = shifted(grad_rows, "feat", 1)

    def halves(weight):
        left, right = weight[:, :half_width], weight[:, half_width:]
        return jnp.where(first, left, right), jnp.where(first, right, left)

    self_w_own, self_w_oth = halves(self_weight)
    neighbor_w_own, neighbor_w_oth = halves(neighbor_weight)
    self_term = jnp.einsum(
        "ro,do->rd", grad_rows, self_w_own, preferred_element_type=F32
    ) + jnp.einsum("ro,do->rd", grad_rows_other, self_w_oth, preferred_element_type=F32)

    products = product(feat_index.reshape(1).astype(jnp.int32), sums, extended, row_devices)
    self_sum, products = lax.optimization_barrier((self_piece, products))
    step = 1
    while 2 * step < row_devices:
        self_sum = exchanged(self_sum, step)
        step *= 2
    products, sums_got, self_sum = lax.optimization_barrier((products, sums_got, self_sum))
    products_got = lax.all_to_all(products, "row", 0, 0)
    if step < row_devices:
        self_sum = exchanged(self_sum, step)

    edge = (local_blocks // rep_devices) * half_width
    summed = sums_got.astype(F32).sum(0)
    from_upper = shifted(summed[:edge], "row", -1)
    from_lower = shifted(summed[2 * edge :], "row", 1)

    product_sum = products_got.astype(F32).sum(0)
    product_hi = product_sum.astype(BF)
    product_lo = (product_sum - product_hi.astype(F32)).astype(BF)
    self_rows = self_sum.astype(BF).reshape(-1, lanes)
    to_all = jnp.concatenate([product_hi, product_lo, self_rows])
    got = lax.all_to_all(
        jnp.broadcast_to(to_all[None], (rep_devices,) + to_all.shape), "rep", 0, 0
    )
    middle = product_sum.shape[0]
    neighbor_piece = (got[:, :middle].astype(F32) + got[:, middle : 2 * middle].astype(F32)).sum(0)
    neighbor_piece = neighbor_piece.reshape(2, chunks, -1, lanes)
    neighbor_grad = whole(collect(neighbor_piece), scaling)

    h_own = (summed[edge : 2 * edge] + from_upper + from_lower).reshape(-1, half_width, lanes)
    h_other = shifted(h_own, "feat", 1)
    features_grad = finish(h_own, h_other, neighbor_w_own, neighbor_w_oth, self_term)

    self_pieces = got[:, 2 * middle :].reshape((rep_devices,) + self_sum.shape)
    keep = jnp.where(first, self_pieces[:, 0], self_pieces[:, 1])
    send = jnp.where(first, self_pieces[:, 1], self_pieces[:, 0])
    came = shifted(send, "feat", 1)
    self_grad = whole(
        jnp.concatenate([jnp.where(first, keep, came), jnp.where(first, came, keep)]), scaling
    )
    return (features_grad, self_grad, neighbor_grad)


def solution(mesh):
    return jax.shard_map(
        local,
        mesh=mesh,
        in_specs=(
            P("row", "feat"),
            P("row", "feat"),
            P("row", "feat"),
            P("row", "rep"),
            P("row"),
            P("row", "rep", None, None),
            P("feat", None),
            P("feat", None),
        ),
        out_specs=(P(("row", "rep"), "feat"), P("feat", None), P("feat", None)),
        check_vma=False,
    )
```

time: 161 us -> 129 us (0.80)
  waiting for transfers between devices: 93.5 us -> 44.6 us
  starting transfers between devices: 35 us -> 50.1 us
  other arithmetic: 2.7 us -> 5.9 us
  Pallas kernels: 18.7 us -> 16.9 us
    all_to_all x5 -> x4, waiting for transfers between devices: 65.2 us -> 30.4 us  [the longest x1 12.3 us: collect(): return lax.all_to_all(sent, ('feat', 'row'), 0, 0)]
    ppermute x5 -> x10, waiting for transfers between devices: 28.3 us -> 6.59 us  [shifted(): lax.ppermute(array, axis, [(i, (i + by) % size) for i in range(size)])]
    ppermute x0 -> x4, starting transfers between devices: none -> 9.27 us  [exchanged(): lax.ppermute(value, 'row', [(i, i ^ step) for i in range(count)])]
    ppermute x0 -> x4, waiting for transfers between devices: none -> 7.67 us  [exchanged(): lax.ppermute(value, 'row', [(i, i ^ step) for i in range(count)])]
    ppermute x5 -> x10, starting transfers between devices: 2.99 us -> 7.02 us  [shifted(): lax.ppermute(array, axis, [(i, (i + by) % size) for i in range(size)])]
    mul x2, other arithmetic: 0.02 us -> 2.38 us  [the longest x1 2.06 us: local(): masked_grad = grad_out * relu_mask.astype(BF)]
    broadcast_in_dim x4 -> x3, local copies, waits for them, and re-layouts: 3.82 us -> 1.91 us  [the longest x2 1.05 us: collect(): sent = jnp.broadcast_to(piece[:, None], (feats, rows) + piece.shape[1:])]
    pallas_call x2, Pallas kernels: 17.5 us -> 15.6 us  [the longest x1 10.3 us: sparse_pass(): pl.pallas_call(sparse_kernel, in_specs=[smem, hbm, vmem], out_specs=vmem,...]
  transfers between devices with their start and end apart: 10 -> 18, of which waited for: 7 -> 11; matrix products, arithmetic and copies ran while one was open for 4% -> 9% of each run, Pallas kernels for 9% -> 13%
where the time goes in v2:
time: 129 us
  starting transfers between devices  50.1 us (39%)
  waiting for transfers between devices  44.6 us (35%)
  Pallas kernels  16.9 us (13%)
  local copies, waits for them, and re-layouts  7.98 us (6%)
  other arithmetic  5.9 us (5%)
  matrix products  2.29 us (2%)
    all_to_all x1, waiting for transfers between devices, collect(): return lax.all_to_all(sent, ('feat', 'row'), 0, 0)  12.3 us
    all_to_all x1, starting transfers between devices, collect(): return lax.all_to_all(sent, ('feat', 'row'), 0, 0)  11.2 us
    pallas_call x1, Pallas kernels, sparse_pass(): pl.pallas_call(sparse_kernel, in_specs=[smem, hbm, vmem], out_specs=vmem,...  10.3 us
    all_to_all x1, starting transfers between devices, local(): products_got = lax.all_to_all(products, 'row', 0, 0)  9.91 us
    ppermute x4, starting transfers between devices, exchanged(): lax.ppermute(value, 'row', [(i, i ^ step) for i in range(count)])  9.27 us
    ppermute x4, waiting for transfers between devices, exchanged(): lax.ppermute(value, 'row', [(i, i ^ step) for i in range(count)])  7.67 us
    ppermute x10, starting transfers between devices, shifted(): lax.ppermute(array, axis, [(i, (i + by) % size) for i in range(size)])  7.02 us
    all_to_all x1, starting transfers between devices, local(): sums_got = lax.all_to_all(sums, 'rep', 0, 0)  6.65 us
  transfers between devices with their start and end apart: 18, of which 11 were waited for; matrix products, arithmetic and copies ran while one was open for 9% of the time, Pallas kernels for 13%

profile of v2, /device:TPU:33, one launch (start us, length us, event | category | flops | bytes accessed | tf_op | source)
XLA Modules:
  0.0 128.7 jit_solution(8834498137823774111)
XLA Ops:
  0.6 0.8 collective-permute-start
  1.4 1.7 %collective-permute-start.1 = (bf16[2048,256]{1,0:T(8,128)(2,1)}, bf16[2048,256]{1,0:T(8,128)(2,1)}, u32[]{:S(2)}, u32[]{:S(2)}) collective-permute-start(bf16[2048,256]{1,0:T(8,128)(2,1)} %refs_2_.1), channel_id=1, source_target_pairs={{0,16},{16,32},{32,48},{48,64},{64,80},{80,96},{96,112},{112,128},... | collective-permute-start | bytes 3145736 | tf_op jit(solution)/shard_map/ppermute | solution.py:15
  3.1 0.8 fusion.15
  3.8 0.1 reshape.48.pos_ref
  3.9 2.1 %convert_multiply_fusion.g_ref = bf16[2048,256]{1,0:T(8,128)(2,1)S(1)} fusion(bf16[2048,256]{1,0:T(8,128)(2,1)} %param.9, s32[2048,256]{1,0:T(8,128)} %param.10), kind=kLoop, calls=%fused_computation.2 | loop fusion | flops 1048576 | bytes 4194304 | tf_op jit(solution)/shard_map/mul | solution.py:202
  6.0 0.5 fusion.18
  6.5 0.5 fusion.19
  7.0 10.3 %shard_map.103.sums_ref = bf16[8,1536,128]{2,1,0:T(8,128)(2,1)S(1)} custom-call(s32[256]{0:T(256)S(1)} %reshape.48.pos_ref, bf16[16,16,128,128]{3,2,1,0:T(8,128)(2,1)} %w_hbm.1, bf16[2048,256]{1,0:T(8,128)(2,1)S(1)} %convert_multiply_fusion.g_ref), custom_call_target="tpu_custom_call" | custom-call | flops 2147483648 | bytes 13631488 | tf_op jit(solution)/shard_map/pallas_call | solution.py:56
  17.3 1.7 %copy-done = bf16[8,1536,128]{2,1,0:T(8,128)(2,1)} copy-done((bf16[8,1536,128]{2,1,0:T(8,128)(2,1)}, bf16[8,1536,128]{2,1,0:T(8,128)(2,1)S(1)}, u32[]{:S(2)}) %copy-start) | copy-done | bytes 3145752
  19.0 6.6 %all-to-all-start = ((bf16[8,1536,128]{2,1,0:T(8,128)(2,1)}), bf16[8,1536,128]{2,1,0:T(8,128)(2,1)}, u32[]{:S(2)}, u32[]{:S(2)}) async-start(bf16[8,1536,128]{2,1,0:T(8,128)(2,1)} %copy-done), calls=%async_computation | async-start | bytes 6291456 | tf_op jit(solution)/shard_map/all_to_all | solution.py:220
  25.6 1.0 collective-permute-done.1.refs_0_
  26.6 1.6 %collective-permute-done.2.refs_4_ = bf16[2048,256]{1,0:T(8,128)(2,1)} collective-permute-done((bf16[2048,256]{1,0:T(8,128)(2,1)}, bf16[2048,256]{1,0:T(8,128)(2,1)}, u32[]{:S(2)}, u32[]{:S(2)}) %collective-permute-start.2) | collective-permute-done | bytes 1048608 | tf_op jit(solution)/shard_map/ppermute | solution.py:15
  28.2 1.0 collective-permute-start.3
  29.2 0.0 collective-permute-start.4
  29.2 2.5 %collective-permute-done.3.refs_1_ = bf16[2048,256]{1,0:T(8,128)(2,1)S(1)} collective-permute-done((bf16[2048,256]{1,0:T(8,128)(2,1)}, bf16[2048,256]{1,0:T(8,128)(2,1)S(1)}, u32[]{:S(2)}, u32[]{:S(2)}) %collective-permute-start.3) | collective-permute-done | bytes 1048608 | tf_op jit(solution)/shard_map/ppermute | solution.py:15
  31.6 1.5 %collective-permute-done.4.refs_5_ = bf16[2048,256]{1,0:T(8,128)(2,1)S(1)} collective-permute-done((bf16[2048,256]{1,0:T(8,128)(2,1)}, bf16[2048,256]{1,0:T(8,128)(2,1)S(1)}, u32[]{:S(2)}, u32[]{:S(2)}) %collective-permute-start.4) | collective-permute-done | bytes 1048608 | tf_op jit(solution)/shard_map/ppermute | solution.py:15
  33.2 1.0 copy-done.4
  34.2 5.4 %shard_map.104 = bf16[16,64,128]{2,1,0:T(8,128)(2,1)} custom-call(s32[1]{0:T(128)} %bitcast.4.feat_ref, bf16[8,1536,128]{2,1,0:T(8,128)(2,1)} %copy-done, bf16[2048,256]{1,0:T(8,128)(2,1)} %collective-permute-done.1.refs_0_, bf16[2048,256]{1,0:T(8,128)(2,1)S(1)} %collective-permute-done.3.refs_1_, bf16[2048,256]{1,0:T(8,128)(2,1)S(1)} %copy-done.1, ...), custom_call_target="tpu_custom_call" | custom-call | flops 12079595520 | bytes 10485760 | tf_op jit(solution)/shard_map/pallas_call | solution.py:112
  39.6 3.0 %collective-permute-start.5 = (f32[2,2,32,128]{3,2,1,0:T(8,128)S(1)}, f32[2,2,32,128]{3,2,1,0:T(8,128)S(1)}, u32[]{:S(2)}, u32[]{:S(2)}) collective-permute-start(f32[2,2,32,128]{3,2,1,0:T(8,128)S(1)} %pad_maximum_fusion), channel_id=1, source_target_pairs={{0,16},{16,0},{32,48},{48,32},{64,80},{80,64},{96,112},{112,96},{1... | collective-permute-start | bytes 196616 | tf_op jit(solution)/shard_map/ppermute | solution.py:153
  42.6 2.3 %collective-permute-done.5 = f32[2,2,32,128]{3,2,1,0:T(8,128)S(1)} collective-permute-done((f32[2,2,32,128]{3,2,1,0:T(8,128)S(1)}, f32[2,2,32,128]{3,2,1,0:T(8,128)S(1)}, u32[]{:S(2)}, u32[]{:S(2)}) %collective-permute-start.5) | collective-permute-done | bytes 65568 | tf_op jit(solution)/shard_map/ppermute | solution.py:153
  44.9 3.5 %collective-permute-start.6 = (f32[2,2,32,128]{3,2,1,0:T(8,128)S(1)}, f32[2,2,32,128]{3,2,1,0:T(8,128)S(1)}, u32[]{:S(2)}, u32[]{:S(2)}) collective-permute-start(f32[2,2,32,128]{3,2,1,0:T(8,128)S(1)} %add.61), channel_id=1, source_target_pairs={{0,32},{16,48},{32,0},{48,16},{64,96},{80,112},{96,64},{112,80},{1... | collective-permute-start | bytes 196616 | tf_op jit(solution)/shard_map/ppermute | solution.py:153
  48.4 1.5 %collective-permute-start.11 = (bf16[256,256]{1,0:T(8,128)(2,1)S(1)}, bf16[256,256]{1,0:T(8,128)(2,1)}, u32[]{:S(2)}, u32[]{:S(2)}) collective-permute-start(bf16[256,256]{1,0:T(8,128)(2,1)S(1)} %constant_dynamic-slice_fusion), channel_id=1, source_target_pairs={{0,1},{1,0},{2,3},{3,2},{4,5},{5,4},{6,7},{7,6},{8,9},{9,8},{10,11... | collective-permute-start | bytes 393224 | tf_op jit(solution)/shard_map/ppermute | solution.py:15
  49.9 0.5 collective-permute-done.6
  50.5 2.4 %collective-permute-start.7 = (f32[2,2,32,128]{3,2,1,0:T(8,128)S(1)}, f32[2,2,32,128]{3,2,1,0:T(8,128)S(1)}, u32[]{:S(2)}, u32[]{:S(2)}) collective-permute-start(f32[2,2,32,128]{3,2,1,0:T(8,128)S(1)} %add.62), channel_id=1, source_target_pairs={{0,64},{16,80},{32,96},{48,112},{64,0},{80,16},{96,32},{112,48},{1... | collective-permute-start | bytes 196616 | tf_op jit(solution)/shard_map/ppermute | solution.py:153
  52.9 0.2 fusion.4
  53.1 4.8 %collective-permute-done.7 = f32[2,2,32,128]{3,2,1,0:T(8,128)S(1)} collective-permute-done((f32[2,2,32,128]{3,2,1,0:T(8,128)S(1)}, f32[2,2,32,128]{3,2,1,0:T(8,128)S(1)}, u32[]{:S(2)}, u32[]{:S(2)}) %collective-permute-start.7) | collective-permute-done | bytes 65568 | tf_op jit(solution)/shard_map/ppermute | solution.py:153
  58.0 5.1 %all-to-all-done = bf16[8,1536,128]{2,1,0:T(8,128)(2,1)} async-done(((bf16[8,1536,128]{2,1,0:T(8,128)(2,1)}), bf16[8,1536,128]{2,1,0:T(8,128)(2,1)}, u32[]{:S(2)}, u32[]{:S(2)}) %all-to-all-start) | async-done | bytes 3145760 | tf_op jit(solution)/shard_map/all_to_all | solution.py:220
  63.1 0.3 collective-permute-start.12
  63.4 9.9 %all-to-all-start.1 = ((bf16[16,64,128]{2,1,0:T(8,128)(2,1)}), bf16[16,64,128]{2,1,0:T(8,128)(2,1)S(1)}, u32[]{:S(2)}, u32[]{:S(2)}) async-start(bf16[16,64,128]{2,1,0:T(8,128)(2,1)} %shard_map.104), calls=%async_computation.1 | async-start | bytes 524288 | tf_op jit(solution)/shard_map/all_to_all | solution.py:246
  73.4 2.4 %convert_reduce_fusion = f32[1536,128]{1,0:T(8,128)S(1)} fusion(bf16[8,1536,128]{2,1,0:T(8,128)(2,1)} %all-to-all-done), kind=kLoop, calls=%fused_computation | loop fusion | flops 2949120 | bytes 3932160 | tf_op jit(solution)/shard_map/reduce_sum | solution.py:251
  75.8 6.3 %all-to-all-done.1 = bf16[16,64,128]{2,1,0:T(8,128)(2,1)S(1)} async-done(((bf16[16,64,128]{2,1,0:T(8,128)(2,1)}), bf16[16,64,128]{2,1,0:T(8,128)(2,1)S(1)}, u32[]{:S(2)}, u32[]{:S(2)}) %all-to-all-start.1) | async-done | bytes 262176 | tf_op jit(solution)/shard_map/all_to_all | solution.py:246
  82.2 0.9 broadcast_in_dim.29
  83.1 6.1 %all-to-all-start.2 = ((bf16[8,256,128]{2,1,0:T(8,128)(2,1)}), bf16[8,256,128]{2,1,0:T(8,128)(2,1)S(1)}, u32[]{:S(2)}, u32[]{:S(2)}) async-start(bf16[8,256,128]{2,1,0:T(8,128)(2,1)} %broadcast_in_dim.29), calls=%async_computation.2 | async-start | bytes 1048576 | tf_op jit(solution)/shard_map/all_to_all | solution.py:260
  89.1 0.7 fusion.17
  89.9 1.5 %collective-permute-start.8 = (f32[512,128]{1,0:T(8,128)S(1)}, f32[512,128]{1,0:T(8,128)S(1)}, u32[]{:S(2)}, u32[]{:S(2)}) collective-permute-start(f32[512,128]{1,0:T(8,128)S(1)} %get-tuple-element.28), channel_id=1, source_target_pairs={{0,240},{16,0},{32,16},{48,32},{64,48},{80,64},{96,80},{112,96},{1... | collective-permute-start | bytes 786440 | tf_op jit(solution)/shard_map/ppermute | solution.py:15
  91.4 6.5 %all-to-all-done.2 = bf16[8,256,128]{2,1,0:T(8,128)(2,1)S(1)} async-done(((bf16[8,256,128]{2,1,0:T(8,128)(2,1)}), bf16[8,256,128]{2,1,0:T(8,128)(2,1)S(1)}, u32[]{:S(2)}, u32[]{:S(2)}) %all-to-all-start.2) | async-done | bytes 524320 | tf_op jit(solution)/shard_map/all_to_all | solution.py:260
  98.0 1.0 broadcast_in_dim.31
  99.0 11.2 %all-to-all-start.3 = ((f32[32,2,16,128]{3,1,2,0:T(2,128)}), f32[32,2,16,128]{3,1,2,0:T(2,128)S(1)}, u32[]{:S(2)}, u32[]{:S(2)}) async-start(f32[32,2,16,128]{3,1,2,0:T(2,128)} %bitcast.15), calls=%async_computation.3 | async-start | bytes 1048576 | tf_op jit(solution)/shard_map/all_to_all | solution.py:166
  110.3 0.4 collective-permute-start.10
  110.7 0.3 collective-permute-start.13
  111.1 1.1 convolution_add_fusion.self_ref
  112.2 1.2 shard_map.105
  113.5 0.1 multiply_bitcast_fusion
  113.5 0.4 copy.17
  114.0 1.0 copy.19
  115.0 12.3 %all-to-all-done.3 = f32[32,2,16,128]{3,1,2,0:T(2,128)S(1)} async-done(((f32[32,2,16,128]{3,1,2,0:T(2,128)}), f32[32,2,16,128]{3,1,2,0:T(2,128)S(1)}, u32[]{:S(2)}, u32[]{:S(2)}) %all-to-all-start.3) | async-done | bytes 524320 | tf_op jit(solution)/shard_map/all_to_all | solution.py:166
  127.3 0.3 broadcast_multiply_fusion
  127.7 1.0 copy.20
  (38 shorter events, 0.4 us)
Async XLA Ops:
  0.6 5.4 %copy-start.1 = (bf16[2048,256]{1,0:T(8,128)(2,1)S(1)}, bf16[2048,256]{1,0:T(8,128)(2,1)}, u32[]{:S(2)}) copy-start(bf16[2048,256]{1,0:T(8,128)(2,1)} %refs_2_.1) | copy-start | bytes 3145732
  0.6 5.8 %collective-permute-start = (bf16[2048,256]{1,0:T(8,128)(2,1)}, bf16[2048,256]{1,0:T(8,128)(2,1)S(1)}, u32[]{:S(2)}, u32[]{:S(2)}) collective-permute-start(bf16[2048,256]{1,0:T(8,128)(2,1)} %refs_2_.1), channel_id=1, source_target_pairs={{0,1},{1,0},{2,3},{3,2},{4,5},{5,4},{6,7},{7,6},{8,9},{9,8},{10,11... | collective-permute-start | bytes 3145736 | tf_op jit(solution)/shard_map/ppermute | solution.py:15
  1.4 25.2 %collective-permute-start.1 = (bf16[2048,256]{1,0:T(8,128)(2,1)}, bf16[2048,256]{1,0:T(8,128)(2,1)}, u32[]{:S(2)}, u32[]{:S(2)}) collective-permute-start(bf16[2048,256]{1,0:T(8,128)(2,1)} %refs_2_.1), channel_id=1, source_target_pairs={{0,16},{16,32},{32,48},{48,64},{64,80},{80,96},{96,112},{112,128},... | collective-permute-start | bytes 3145736 | tf_op jit(solution)/shard_map/ppermute | solution.py:15
  3.1 25.1 %collective-permute-start.2 = (bf16[2048,256]{1,0:T(8,128)(2,1)}, bf16[2048,256]{1,0:T(8,128)(2,1)}, u32[]{:S(2)}, u32[]{:S(2)}) collective-permute-start(bf16[2048,256]{1,0:T(8,128)(2,1)} %refs_2_.1), channel_id=1, source_target_pairs={{0,240},{16,0},{32,16},{48,32},{64,48},{80,64},{96,80},{112,96},{1... | collective-permute-start | bytes 3145736 | tf_op jit(solution)/shard_map/ppermute | solution.py:15
  17.3 1.7 %copy-start = (bf16[8,1536,128]{2,1,0:T(8,128)(2,1)}, bf16[8,1536,128]{2,1,0:T(8,128)(2,1)S(1)}, u32[]{:S(2)}) copy-start(bf16[8,1536,128]{2,1,0:T(8,128)(2,1)S(1)} %shard_map.103.sums_ref) | copy-start | bytes 9437188
  19.0 44.2 %all-to-all-start = ((bf16[8,1536,128]{2,1,0:T(8,128)(2,1)}), bf16[8,1536,128]{2,1,0:T(8,128)(2,1)}, u32[]{:S(2)}, u32[]{:S(2)}) async-start(bf16[8,1536,128]{2,1,0:T(8,128)(2,1)} %copy-done), calls=%async_computation | async-start | bytes 6291456 | tf_op jit(solution)/shard_map/all_to_all | solution.py:220
  28.2 3.5 %collective-permute-start.3 = (bf16[2048,256]{1,0:T(8,128)(2,1)}, bf16[2048,256]{1,0:T(8,128)(2,1)S(1)}, u32[]{:S(2)}, u32[]{:S(2)}) collective-permute-start(bf16[2048,256]{1,0:T(8,128)(2,1)} %collective-permute-done.1.refs_0_), channel_id=1, source_target_pairs={{0,1},{1,0},{2,3},{3,2},{4,5},{5,4},{6,7},{7,6},{8,9},{9,8},{10,11... | collective-permute-start | bytes 3145736 | tf_op jit(solution)/shard_map/ppermute | solution.py:15
  29.2 4.0 %collective-permute-start.4 = (bf16[2048,256]{1,0:T(8,128)(2,1)}, bf16[2048,256]{1,0:T(8,128)(2,1)S(1)}, u32[]{:S(2)}, u32[]{:S(2)}) collective-permute-start(bf16[2048,256]{1,0:T(8,128)(2,1)} %collective-permute-done.2.refs_4_), channel_id=1, source_target_pairs={{0,1},{1,0},{2,3},{3,2},{4,5},{5,4},{6,7},{7,6},{8,9},{9,8},{10,11... | collective-permute-start | bytes 3145736 | tf_op jit(solution)/shard_map/ppermute | solution.py:15
  33.1 1.0 copy-start.4
  34.2 18.7 %copy-start.3 = (bf16[256,512]{1,0:T(8,128)(2,1)S(1)}, bf16[256,512]{1,0:T(8,128)(2,1)}, u32[]{:S(2)}) copy-start(bf16[256,512]{1,0:T(8,128)(2,1)} %param.14) | copy-start | bytes 786436
  39.6 5.3 %collective-permute-start.5 = (f32[2,2,32,128]{3,2,1,0:T(8,128)S(1)}, f32[2,2,32,128]{3,2,1,0:T(8,128)S(1)}, u32[]{:S(2)}, u32[]{:S(2)}) collective-permute-start(f32[2,2,32,128]{3,2,1,0:T(8,128)S(1)} %pad_maximum_fusion), channel_id=1, source_target_pairs={{0,16},{16,0},{32,48},{48,32},{64,80},{80,64},{96,112},{112,96},{1... | collective-permute-start | bytes 196616 | tf_op jit(solution)/shard_map/ppermute | solution.py:153
  44.9 5.5 %collective-permute-start.6 = (f32[2,2,32,128]{3,2,1,0:T(8,128)S(1)}, f32[2,2,32,128]{3,2,1,0:T(8,128)S(1)}, u32[]{:S(2)}, u32[]{:S(2)}) collective-permute-start(f32[2,2,32,128]{3,2,1,0:T(8,128)S(1)} %add.61), channel_id=1, source_target_pairs={{0,32},{16,48},{32,0},{48,16},{64,96},{80,112},{96,64},{112,80},{1... | collective-permute-start | bytes 196616 | tf_op jit(solution)/shard_map/ppermute | solution.py:153
  48.4 62.6 %collective-permute-start.11 = (bf16[256,256]{1,0:T(8,128)(2,1)S(1)}, bf16[256,256]{1,0:T(8,128)(2,1)}, u32[]{:S(2)}, u32[]{:S(2)}) collective-permute-start(bf16[256,256]{1,0:T(8,128)(2,1)S(1)} %constant_dynamic-slice_fusion), channel_id=1, source_target_pairs={{0,1},{1,0},{2,3},{3,2},{4,5},{5,4},{6,7},{7,6},{8,9},{9,8},{10,11... | collective-permute-start | bytes 393224 | tf_op jit(solution)/shard_map/ppermute | solution.py:15
  50.5 7.5 %collective-permute-start.7 = (f32[2,2,32,128]{3,2,1,0:T(8,128)S(1)}, f32[2,2,32,128]{3,2,1,0:T(8,128)S(1)}, u32[]{:S(2)}, u32[]{:S(2)}) collective-permute-start(f32[2,2,32,128]{3,2,1,0:T(8,128)S(1)} %add.62), channel_id=1, source_target_pairs={{0,64},{16,80},{32,96},{48,112},{64,0},{80,16},{96,32},{112,48},{1... | collective-permute-start | bytes 196616 | tf_op jit(solution)/shard_map/ppermute | solution.py:153
  63.1 12.7 %collective-permute-start.12 = (f32[2,2,32,128]{3,2,1,0:T(8,128)S(1)}, f32[2,2,32,128]{3,2,1,0:T(8,128)S(1)}, u32[]{:S(2)}, u32[]{:S(2)}) collective-permute-start(f32[2,2,32,128]{3,2,1,0:T(8,128)S(1)} %add.63), channel_id=1, source_target_pairs={{0,128},{16,144},{32,160},{48,176},{64,192},{80,208},{96,224},{112... | collective-permute-start | bytes 196616 | tf_op jit(solution)/shard_map/ppermute | solution.py:153
  63.4 18.7 %all-to-all-start.1 = ((bf16[16,64,128]{2,1,0:T(8,128)(2,1)}), bf16[16,64,128]{2,1,0:T(8,128)(2,1)S(1)}, u32[]{:S(2)}, u32[]{:S(2)}) async-start(bf16[16,64,128]{2,1,0:T(8,128)(2,1)} %shard_map.104), calls=%async_computation.1 | async-start | bytes 524288 | tf_op jit(solution)/shard_map/all_to_all | solution.py:246
  73.3 18.0 %copy-start.2 = (bf16[256,512]{1,0:T(8,128)(2,1)S(1)}, bf16[256,512]{1,0:T(8,128)(2,1)}, u32[]{:S(2)}) copy-start(bf16[256,512]{1,0:T(8,128)(2,1)} %param.15) | copy-start | bytes 786436
  83.1 14.8 %all-to-all-start.2 = ((bf16[8,256,128]{2,1,0:T(8,128)(2,1)}), bf16[8,256,128]{2,1,0:T(8,128)(2,1)S(1)}, u32[]{:S(2)}, u32[]{:S(2)}) async-start(bf16[8,256,128]{2,1,0:T(8,128)(2,1)} %broadcast_in_dim.29), calls=%async_computation.2 | async-start | bytes 1048576 | tf_op jit(solution)/shard_map/all_to_all | solution.py:260
  89.9 20.4 %collective-permute-start.9 = (f32[512,128]{1,0:T(8,128)}, f32[512,128]{1,0:T(8,128)S(1)}, u32[]{:S(2)}, u32[]{:S(2)}) collective-permute-start(f32[512,128]{1,0:T(8,128)} %get-tuple-element.29), channel_id=1, source_target_pairs={{0,16},{16,32},{32,48},{48,64},{64,80},{80,96},{96,112},{112,128},... | collective-permute-start | bytes 786440 | tf_op jit(solution)/shard_map/ppermute | solution.py:15
  89.9 20.4 %collective-permute-start.8 = (f32[512,128]{1,0:T(8,128)S(1)}, f32[512,128]{1,0:T(8,128)S(1)}, u32[]{:S(2)}, u32[]{:S(2)}) collective-permute-start(f32[512,128]{1,0:T(8,128)S(1)} %get-tuple-element.28), channel_id=1, source_target_pairs={{0,240},{16,0},{32,16},{48,32},{64,48},{80,64},{96,80},{112,96},{1... | collective-permute-start | bytes 786440 | tf_op jit(solution)/shard_map/ppermute | solution.py:15
  99.0 28.3 %all-to-all-start.3 = ((f32[32,2,16,128]{3,1,2,0:T(2,128)}), f32[32,2,16,128]{3,1,2,0:T(2,128)S(1)}, u32[]{:S(2)}, u32[]{:S(2)}) async-start(f32[32,2,16,128]{3,1,2,0:T(2,128)} %bitcast.15), calls=%async_computation.3 | async-start | bytes 1048576 | tf_op jit(solution)/shard_map/all_to_all | solution.py:166
  110.3 1.9 %collective-permute-start.10 = (f32[2,256,128]{2,1,0:T(8,128)S(1)}, f32[2,256,128]{2,1,0:T(8,128)S(1)}, u32[]{:S(2)}, u32[]{:S(2)}) collective-permute-start(f32[2,256,128]{2,1,0:T(8,128)S(1)} %bitcast.73), channel_id=1, source_target_pairs={{0,1},{1,0},{2,3},{3,2},{4,5},{5,4},{6,7},{7,6},{8,9},{9,8},{10,11... | collective-permute-start | bytes 786440 | tf_op jit(solution)/shard_map/ppermute | solution.py:15
  110.7 2.7 %collective-permute-start.13 = (bf16[8,2,32,128]{3,2,1,0:T(8,128)(2,1)S(1)}, bf16[8,2,32,128]{3,2,1,0:T(8,128)(2,1)S(1)}, u32[]{:S(2)}, u32[]{:S(2)}) collective-permute-start(bf16[8,2,32,128]{3,2,1,0:T(8,128)(2,1)S(1)} %fusion.1), channel_id=1, source_target_pairs={{0,1},{1,0},{2,3},{3,2},{4,5},{5,4},{6,7},{7,6},{8,9},{9,8},{10,11... | collective-permute-start | bytes 393224 | tf_op jit(solution)/shard_map/ppermute | solution.py:15

commit v3 on v2

--- a/solution.py
+++ b/solution.py
@@ -16,7 +16,7 @@
 
 
 def sparse_kernel(
-    pos_ref, w_hbm, g_ref, out_ref, acc_ref, w_ref, wsem
+    pos_ref, w_hbm, g_ref, sides_ref, own_ref, acc_ref, w_ref, wsem
 ):
     blocks, slots, size, _ = w_hbm.shape
 
@@ -39,11 +39,11 @@
             acc_ref[pos_ref[b * slots + s + 1]] += terms[:, size:]
 
     width = g_ref.shape[1]
-    pieces = blocks // out_ref.shape[0]
-    for side in range(3):
-        for b in range(blocks):
-            at = (side * pieces + b % pieces) * width
-            out_ref[b // pieces, at : at + width, :] = acc_ref[side * blocks + b].astype(BF)
+    pieces = blocks // own_ref.shape[0]
+    for b in range(blocks):
+        at = (b % pieces) * width
+        for side, ref, to in ((0, sides_ref, at), (1, own_ref, at), (2, sides_ref, pieces * width + at)):
+            ref[b // pieces, to : to + width, :] = acc_ref[side * blocks + b].astype(BF)
 
 
 def sparse_pass(destinations, weights, grad, parts):
@@ -56,8 +56,11 @@
     return pl.pallas_call(
         sparse_kernel,
         in_specs=[smem, hbm, vmem],
-        out_specs=vmem,
-        out_shape=jax.ShapeDtypeStruct((parts, 3 * pieces * width, size), BF),
+        out_specs=[vmem] * 2,
+        out_shape=[
+            jax.ShapeDtypeStruct((parts, 2 * pieces * width, size), BF),
+            jax.ShapeDtypeStruct((parts, pieces * width, size), BF),
+        ],
         scratch_shapes=[
             pltpu.VMEM((3 * blocks + 1, width, size), F32),
             pltpu.VMEM(weights.shape, BF),
@@ -72,21 +75,30 @@
     )(destinations, weights, grad)
 
 
-def product_kernel(feat_ref, sums_ref, *refs):
-    f_refs, out_ref, h_ref = refs[:6], refs[6], refs[7]
-    parts, depth, size = sums_ref.shape
-    width = f_refs[0].shape[1]
-    pieces = depth // (3 * width)
-    for side in range(3):
+def product_kernel(feat_ref, own_hbm, sides_hbm, *refs):
+    f_hbm, (out_ref, own_ref, sides_ref, h_ref, f_ref, sem) = refs[:6], refs[6:]
+    ends = [(own_hbm, own_ref), (sides_hbm, sides_ref)]
+    ends += [(f_hbm[i], f_ref.at[i]) for i in range(6)]
+    copies = [pltpu.make_async_copy(a, b, sem.at[i]) for i, (a, b) in enumerate(ends)]
+    for copy in copies:
+        copy.start()
+    parts, edge, size = own_ref.shape
+    width = f_ref.shape[2]
+    pieces = edge // width
+    copies[0].wait()
+    copies[1].wait()
+    for side, ref, base in ((0, sides_ref, 0), (1, own_ref, 0), (2, sides_ref, edge)):
         for b in range(parts * pieces):
-            at = (side * pieces + b % pieces) * width
-            h_ref[side, :, b * size : (b + 1) * size] = sums_ref[b // pieces, at : at + width, :]
+            at = base + (b % pieces) * width
+            h_ref[side, :, b * size : (b + 1) * size] = ref[b // pieces, at : at + width, :]
+    for copy in copies[2:]:
+        copy.wait()
     products = []
     for which in range(2):
         total = jnp.zeros((width, width), F32)
         for side in range(3):
             total += jnp.dot(
-                h_ref[side], f_refs[side * 2 + which][...], preferred_element_type=F32
+                h_ref[side], f_ref[side * 2 + which], preferred_element_type=F32
             )
         products.append(total)
     first = feat_ref[0] == 0
@@ -103,23 +115,30 @@
                 ]
 
 
-def product(feat_index, sums, features, targets):
-    size = sums.shape[2]
+def product(feat_index, own, sides, features, targets):
+    size = own.shape[2]
     rows, width = features[0].shape
     vmem = pl.BlockSpec(memory_space=pltpu.VMEM)
     smem = pl.BlockSpec(memory_space=pltpu.SMEM)
+    hbm = pl.BlockSpec(memory_space=pltpu.HBM)
     depth = 2 * (width // size) * (width // targets)
     return pl.pallas_call(
         product_kernel,
-        in_specs=[smem] + [vmem] * (1 + len(features)),
+        in_specs=[smem] + [hbm] * (2 + len(features)),
         out_specs=vmem,
         out_shape=jax.ShapeDtypeStruct((targets, depth, size), BF),
-        scratch_shapes=[pltpu.VMEM((3, width, rows), BF)],
+        scratch_shapes=[
+            pltpu.VMEM(own.shape, BF),
+            pltpu.VMEM(sides.shape, BF),
+            pltpu.VMEM((3, width, rows), BF),
+            pltpu.VMEM((len(features), rows, width), BF),
+            pltpu.SemaphoreType.DMA((2 + len(features),)),
+        ],
         compiler_params=pltpu.CompilerParams(vmem_limit_bytes=VMEM_LIMIT),
         cost_estimate=pl.CostEstimate(
-            flops=90 * rows * width * width, bytes_accessed=10 * 2**20, transcendentals=0
+            flops=12 * rows * width * width, bytes_accessed=10 * 2**20, transcendentals=0
         ),
-    )(feat_index, sums, *features)
+    )(feat_index, own, sides, *features)
 
 
 def finish_kernel(own_ref, oth_ref, wown_ref, woth_ref, self_ref, out_ref):
@@ -216,9 +235,17 @@
         [jnp.where(first, self_own, self_oth), jnp.where(first, self_oth, self_own)]
     )
     self_piece, grad_values = lax.optimization_barrier((self_piece, masked_grad))
-    sums = sparse_pass(destinations, block_weights, grad_values, rep_devices)
-    sums_got = lax.all_to_all(sums, "rep", 0, 0)
-    before, after, sums = lax.optimization_barrier((before, after, sums))
+    sides, own = sparse_pass(destinations, block_weights, grad_values, rep_devices)
+    sides_got = lax.all_to_all(sides, "rep", 0, 0)
+    before, after, own = lax.optimization_barrier((before, after, own))
+    self_sum, step = self_piece, 1
+    while 4 * step < row_devices:
+        self_sum = exchanged(self_sum, step)
+        step *= 2
+    self_sum, own = lax.optimization_barrier((self_sum, own))
+    if 2 * step < row_devices:
+        self_sum = exchanged(self_sum, step)
+        step *= 2
     extended = []
     for rows, other in ((before, None), (features, features_other), (after, None)):
         extended += [rows, shifted(rows, "feat", 1) if other is None else other]
@@ -236,40 +263,39 @@
         "ro,do->rd", grad_rows, self_w_own, preferred_element_type=F32
     ) + jnp.einsum("ro,do->rd", grad_rows_other, self_w_oth, preferred_element_type=F32)
 
-    products = product(feat_index.reshape(1).astype(jnp.int32), sums, extended, row_devices)
-    self_sum, products = lax.optimization_barrier((self_piece, products))
-    step = 1
-    while 2 * step < row_devices:
-        self_sum = exchanged(self_sum, step)
-        step *= 2
-    products, sums_got, self_sum = lax.optimization_barrier((products, sums_got, self_sum))
+    products = product(
+        feat_index.reshape(1).astype(jnp.int32), own, sides, extended, row_devices
+    )
+    products, sides_got, self_sum = lax.optimization_barrier((products, sides_got, self_sum))
     products_got = lax.all_to_all(products, "row", 0, 0)
     if step < row_devices:
         self_sum = exchanged(self_sum, step)
 
     edge = (local_blocks // rep_devices) * half_width
-    summed = sums_got.astype(F32).sum(0)
-    from_upper = shifted(summed[:edge], "row", -1)
-    from_lower = shifted(summed[2 * edge :], "row", 1)
+    sides_sum = sides_got.astype(F32).sum(0).astype(BF)
+    from_upper = shifted(sides_sum[:edge], "row", -1)
+    from_lower = shifted(sides_sum[edge:], "row", 1)
 
     product_sum = products_got.astype(F32).sum(0)
-    product_hi = product_sum.astype(BF)
-    product_lo = (product_sum - product_hi.astype(F32)).astype(BF)
+    product_hi = lax.reduce_precision(product_sum, 8, 7)
+    product_lo = (product_sum - product_hi).astype(BF)
     self_rows = self_sum.astype(BF).reshape(-1, lanes)
-    to_all = jnp.concatenate([product_hi, product_lo, self_rows])
-    got = lax.all_to_all(
-        jnp.broadcast_to(to_all[None], (rep_devices,) + to_all.shape), "rep", 0, 0
-    )
-    middle = product_sum.shape[0]
-    neighbor_piece = (got[:, :middle].astype(F32) + got[:, middle : 2 * middle].astype(F32)).sum(0)
+    to_all = jnp.concatenate([product_hi.astype(BF), product_lo, self_rows])
+    to_all = jnp.broadcast_to(to_all[None], (rep_devices,) + to_all.shape)
+    got = lax.all_to_all(jnp.concatenate([own, to_all], axis=1), "rep", 0, 0)
+    middle = edge + product_sum.shape[0]
+    end = middle + product_sum.shape[0]
+    neighbor_piece = (got[:, edge:middle].astype(F32) + got[:, middle:end].astype(F32)).sum(0)
     neighbor_piece = neighbor_piece.reshape(2, chunks, -1, lanes)
     neighbor_grad = whole(collect(neighbor_piece), scaling)
 
-    h_own = (summed[edge : 2 * edge] + from_upper + from_lower).reshape(-1, half_width, lanes)
+    summed = got[:, :edge].astype(F32).sum(0)
+    h_own = summed + from_upper.astype(F32) + from_lower.astype(F32)
+    h_own = h_own.reshape(-1, half_width, lanes)
     h_other = shifted(h_own, "feat", 1)
     features_grad = finish(h_own, h_other, neighbor_w_own, neighbor_w_oth, self_term)
 
-    self_pieces = got[:, 2 * middle :].reshape((rep_devices,) + self_sum.shape)
+    self_pieces = got[:, end:].reshape((rep_devices,) + self_sum.shape)
     keep = jnp.where(first, self_pieces[:, 0], self_pieces[:, 1])
     send = jnp.where(first, self_pieces[:, 1], self_pieces[:, 0])
     came = shifted(send, "feat", 1)

time: 129 us -> 126 us (0.977)
  waiting for transfers between devices: 44.6 us -> 38.7 us
  starting transfers between devices: 50.1 us -> 52.6 us
  other arithmetic: 5.9 us -> 7.8 us
  local copies, waits for them, and re-layouts: 7.98 us -> 6.1 us
    all_to_all x2, waiting for transfers between devices: 11.7 us -> 6.23 us  [the longest x1 6.23 us: local(): got = lax.all_to_all(jnp.concatenate([own, to_all], axis=1), 'rep', 0, 0)]
    all_to_all x1, starting transfers between devices: 9.91 us -> 6.19 us  [local(): products_got = lax.all_to_all(products, 'row', 0, 0)]
    ppermute x4, waiting for transfers between devices: 7.67 us -> 11.3 us  [exchanged(): lax.ppermute(value, 'row', [(i, i ^ step) for i in range(count)])]
    ppermute x10, starting transfers between devices: 7.02 us -> 10.5 us  [shifted(): lax.ppermute(array, axis, [(i, (i + by) % size) for i in range(size)])]
    ppermute x10, waiting for transfers between devices: 6.59 us -> 3.74 us  [shifted(): lax.ppermute(array, axis, [(i, (i + by) % size) for i in range(size)])]
    all_to_all x1, waiting for transfers between devices: 6.34 us -> 4.91 us  [local(): products_got = lax.all_to_all(products, 'row', 0, 0)]
    all_to_all x1, starting transfers between devices: 11.2 us -> 12.5 us  [collect(): return lax.all_to_all(sent, ('feat', 'row'), 0, 0)]
    unnamed x14 -> x16, local copies, waits for them, and re-layouts: 4.81 us -> 4.78 us
  transfers between devices with their start and end apart: 18 -> 18, of which waited for: 11 -> 11; matrix products, arithmetic and copies ran while one was open for 9% -> 8% of each run, Pallas kernels for 13% -> 14%
where the time goes in v3:
time: 126 us; the launch traced here: 125 us
  starting transfers between devices  52.6 us (42%)
  waiting for transfers between devices  38.7 us (31%)
  Pallas kernels  17.9 us (14%)
  other arithmetic  7.8 us (6%)
  local copies, waits for them, and re-layouts  6.1 us (5%)
  matrix products  1.38 us (1%)
    all_to_all x1, starting transfers between devices, collect(): return lax.all_to_all(sent, ('feat', 'row'), 0, 0)  12.5 us
    all_to_all x1, waiting for transfers between devices, collect(): return lax.all_to_all(sent, ('feat', 'row'), 0, 0)  12.5 us
    pallas_call x1, Pallas kernels, sparse_pass(): pl.pallas_call(sparse_kernel, in_specs=[smem, hbm, vmem], out_specs=[vmem...  11.5 us
    ppermute x4, waiting for transfers between devices, exchanged(): lax.ppermute(value, 'row', [(i, i ^ step) for i in range(count)])  11.3 us
    ppermute x10, starting transfers between devices, shifted(): lax.ppermute(array, axis, [(i, (i + by) % size) for i in range(size)])  10.5 us
    ppermute x4, starting transfers between devices, exchanged(): lax.ppermute(value, 'row', [(i, i ^ step) for i in range(count)])  10.3 us
    all_to_all x1, starting transfers between devices, local(): sides_got = lax.all_to_all(sides, 'rep', 0, 0)  6.66 us
    all_to_all x1, starting transfers between devices, local(): got = lax.all_to_all(jnp.concatenate([own, to_all], axis=1), 'rep', 0, 0)  6.46 us
  transfers between devices with their start and end apart: 18, of which 11 were waited for; matrix products, arithmetic and copies ran while one was open for 8% of the time, Pallas kernels for 14%

profile of v3, /device:TPU:33, one launch (start us, length us, event | category | flops | bytes accessed | tf_op | source)
XLA Modules:
  0.0 125.4 jit_solution(3060001045352084375)
XLA Ops:
  0.6 0.8 collective-permute-start
  1.4 1.7 %collective-permute-start.3 = (bf16[2048,256]{1,0:T(8,128)(2,1)}, bf16[2048,256]{1,0:T(8,128)(2,1)}, u32[]{:S(2)}, u32[]{:S(2)}) collective-permute-start(bf16[2048,256]{1,0:T(8,128)(2,1)} %refs_2_.1), channel_id=1, source_target_pairs={{0,16},{16,32},{32,48},{48,64},{64,80},{80,96},{96,112},{112,128},... | collective-permute-start | bytes 3145736 | tf_op jit(solution)/shard_map/ppermute | solution.py:15
  3.1 0.8 fusion.15
  3.9 2.1 %convert_multiply_fusion.g_ref = bf16[2048,256]{1,0:T(8,128)(2,1)S(1)} fusion(bf16[2048,256]{1,0:T(8,128)(2,1)} %param.9, s32[2048,256]{1,0:T(8,128)} %param.10), kind=kLoop, calls=%fused_computation.3 | loop fusion | flops 1048576 | bytes 4194304 | tf_op jit(solution)/shard_map/mul | solution.py:221
  6.1 0.5 fusion.19
  6.6 0.5 fusion.20
  7.1 0.4 copy-done.1
  7.6 11.5 %shard_map.103 = (bf16[8,1024,128]{2,1,0:T(8,128)(2,1)}, bf16[8,512,128]{2,1,0:T(8,128)(2,1)S(1)}) custom-call(s32[256]{0:T(256)S(1)} %reshape.47.pos_ref, bf16[16,16,128,128]{3,2,1,0:T(8,128)(2,1)} %w_hbm.1, bf16[2048,256]{1,0:T(8,128)(2,1)S(1)} %convert_multiply_fusion.g_ref), custom_call_target="tpu_custom_call" | custom-call | flops 2147483648 | bytes 13631488 | tf_op jit(solution)/shard_map/pallas_call | solution.py:56
  19.0 6.7 %all-to-all-start = ((bf16[8,1024,128]{2,1,0:T(8,128)(2,1)}), bf16[8,1024,128]{2,1,0:T(8,128)(2,1)}, u32[]{:S(2)}, u32[]{:S(2)}) async-start(bf16[8,1024,128]{2,1,0:T(8,128)(2,1)} %get-tuple-element.20.sides_hbm), calls=%async_computation | async-start | bytes 4194304 | tf_op jit(solution)/shard_map/all_to_all | solution.py:239
  25.7 0.9 collective-permute-done.3.refs_0_
  26.6 1.6 %collective-permute-done.4.refs_4_ = bf16[2048,256]{1,0:T(8,128)(2,1)} collective-permute-done((bf16[2048,256]{1,0:T(8,128)(2,1)}, bf16[2048,256]{1,0:T(8,128)(2,1)}, u32[]{:S(2)}, u32[]{:S(2)}) %collective-permute-start.4) | collective-permute-done | bytes 1048608 | tf_op jit(solution)/shard_map/ppermute | solution.py:15
  28.2 1.0 collective-permute-start.5
  29.1 3.0 %collective-permute-start.1 = (f32[2,2,32,128]{3,1,2,0:T(2,128)S(1)}, f32[2,2,32,128]{3,1,2,0:T(2,128)S(1)}, u32[]{:S(2)}, u32[]{:S(2)}) collective-permute-start(f32[2,2,32,128]{3,1,2,0:T(2,128)S(1)} %pad_maximum_fusion.1), channel_id=1, source_target_pairs={{0,16},{16,0},{32,48},{48,32},{64,80},{80,64},{96,112},{112,96},{1... | collective-permute-start | bytes 196616 | tf_op jit(solution)/shard_map/ppermute | solution.py:172
  32.2 2.1 %collective-permute-done.1 = f32[2,2,32,128]{3,1,2,0:T(2,128)S(1)} collective-permute-done((f32[2,2,32,128]{3,1,2,0:T(2,128)S(1)}, f32[2,2,32,128]{3,1,2,0:T(2,128)S(1)}, u32[]{:S(2)}, u32[]{:S(2)}) %collective-permute-start.1) | collective-permute-done | bytes 65568 | tf_op jit(solution)/shard_map/ppermute | solution.py:172
  34.3 3.7 %collective-permute-start.2 = (f32[2,2,32,128]{3,1,2,0:T(2,128)S(1)}, f32[2,2,32,128]{3,1,2,0:T(2,128)S(1)}, u32[]{:S(2)}, u32[]{:S(2)}) collective-permute-start(f32[2,2,32,128]{3,1,2,0:T(2,128)S(1)} %add.56), channel_id=1, source_target_pairs={{0,32},{16,48},{32,0},{48,16},{64,96},{80,112},{96,64},{112,80},{1... | collective-permute-start | bytes 196616 | tf_op jit(solution)/shard_map/ppermute | solution.py:172
  38.0 2.1 %collective-permute-done.2 = f32[2,2,32,128]{3,1,2,0:T(2,128)S(1)} collective-permute-done((f32[2,2,32,128]{3,1,2,0:T(2,128)S(1)}, f32[2,2,32,128]{3,1,2,0:T(2,128)S(1)}, u32[]{:S(2)}, u32[]{:S(2)}) %collective-permute-start.2) | collective-permute-done | bytes 65568 | tf_op jit(solution)/shard_map/ppermute | solution.py:172
  40.1 2.4 %collective-permute-start.7 = (f32[2,2,32,128]{3,1,2,0:T(2,128)S(1)}, f32[2,2,32,128]{3,1,2,0:T(2,128)S(1)}, u32[]{:S(2)}, u32[]{:S(2)}) collective-permute-start(f32[2,2,32,128]{3,1,2,0:T(2,128)S(1)} %add.57), channel_id=1, source_target_pairs={{0,64},{16,80},{32,96},{48,112},{64,0},{80,16},{96,32},{112,48},{1... | collective-permute-start | bytes 196616 | tf_op jit(solution)/shard_map/ppermute | solution.py:172
  42.5 5.1 %collective-permute-done.7 = f32[2,2,32,128]{3,1,2,0:T(2,128)S(1)} collective-permute-done((f32[2,2,32,128]{3,1,2,0:T(2,128)S(1)}, f32[2,2,32,128]{3,1,2,0:T(2,128)S(1)}, u32[]{:S(2)}, u32[]{:S(2)}) %collective-permute-start.7) | collective-permute-done | bytes 65568 | tf_op jit(solution)/shard_map/ppermute | solution.py:172
  47.7 1.0 copy-done.3
  48.7 1.2 copy-done.2
  49.9 5.2 %shard_map.104 = bf16[16,64,128]{2,1,0:T(8,128)(2,1)} custom-call(s32[1]{0:T(128)} %bitcast.4.feat_ref, bf16[8,512,128]{2,1,0:T(8,128)(2,1)S(1)} %get-tuple-element.19.own_hbm, bf16[8,1024,128]{2,1,0:T(8,128)(2,1)} %get-tuple-element.20.sides_hbm, bf16[2048,256]{1,0:T(8,128)(2,1)} %collective-permute-done.3.refs_0_, ...), custom_call_target="tpu_custom_call" | custom-call | flops 1610612736 | bytes 10485760 | tf_op jit(solution)/shard_map/pallas_call | solution.py:125
  55.1 6.2 %all-to-all-start.1 = ((bf16[16,64,128]{2,1,0:T(8,128)(2,1)}), bf16[16,64,128]{2,1,0:T(8,128)(2,1)S(1)}, u32[]{:S(2)}, u32[]{:S(2)}) async-start(bf16[16,64,128]{2,1,0:T(8,128)(2,1)} %shard_map.104), calls=%async_computation.1 | async-start | bytes 524288 | tf_op jit(solution)/shard_map/all_to_all | solution.py:270
  61.3 1.2 collective-permute-start.8
  62.5 2.0 %collective-permute-done.8 = f32[2,2,32,128]{3,1,2,0:T(2,128)S(1)} collective-permute-done((f32[2,2,32,128]{3,1,2,0:T(2,128)S(1)}, f32[2,2,32,128]{3,1,2,0:T(2,128)S(1)}, u32[]{:S(2)}, u32[]{:S(2)}) %collective-permute-start.8) | collective-permute-done | bytes 65568 | tf_op jit(solution)/shard_map/ppermute | solution.py:172
  64.6 4.9 %all-to-all-done.1 = bf16[16,64,128]{2,1,0:T(8,128)(2,1)S(1)} async-done(((bf16[16,64,128]{2,1,0:T(8,128)(2,1)}), bf16[16,64,128]{2,1,0:T(8,128)(2,1)S(1)}, u32[]{:S(2)}, u32[]{:S(2)}) %all-to-all-start.1) | async-done | bytes 262176 | tf_op jit(solution)/shard_map/all_to_all | solution.py:270
  69.6 1.2 pad_maximum_fusion
  70.9 6.5 %all-to-all-start.2 = ((bf16[8,768,128]{2,1,0:T(8,128)(2,1)}), bf16[8,768,128]{2,1,0:T(8,128)(2,1)S(1)}, u32[]{:S(2)}, u32[]{:S(2)}) async-start(bf16[8,768,128]{2,1,0:T(8,128)(2,1)} %pad_maximum_fusion), calls=%async_computation.2 | async-start | bytes 3145728 | tf_op jit(solution)/shard_map/all_to_all | solution.py:285
  77.4 4.7 %collective-permute-start.12 = (bf16[256,256]{1,0:T(8,128)(2,1)S(1)}, bf16[256,256]{1,0:T(8,128)(2,1)S(1)}, u32[]{:S(2)}, u32[]{:S(2)}) collective-permute-start(bf16[256,256]{1,0:T(8,128)(2,1)S(1)} %constant_dynamic-slice_fusion), channel_id=1, source_target_pairs={{0,1},{1,0},{2,3},{3,2},{4,5},{5,4},{6,7},{7,6},{8,9},{9,8},{10,11... | collective-permute-start | bytes 393224 | tf_op jit(solution)/shard_map/ppermute | solution.py:15
  82.1 0.2 fusion.3
  82.3 0.7 collective-permute-done.12
  83.1 0.2 convolution_add_fusion.self_ref
  83.3 2.0 %reduce_sum.41 = bf16[1024,128]{1,0:T(8,128)(2,1)S(1)} reduce(bf16[8,1024,128]{2,1,0:T(8,128)(2,1)} %all-to-all-done, bf16[]{:T(256)} %constant.65.clone.1), dimensions={0}, to_apply=%region_2.3 | reduce | flops 917504 | bytes 2359298 | tf_op jit(solution)/shard_map/reduce_sum | solution.py:275
  85.3 0.4 collective-permute-start.10
  85.7 1.3 %collective-permute-start.9 = (bf16[512,128]{1,0:T(8,128)(2,1)S(1)}, bf16[512,128]{1,0:T(8,128)(2,1)S(1)}, u32[]{:S(2)}, u32[]{:S(2)}) collective-permute-start(bf16[512,128]{1,0:T(8,128)(2,1)S(1)} %get-tuple-element.38), channel_id=1, source_target_pairs={{0,240},{16,0},{32,16},{48,32},{64,48},{80,64},{96,80},{112,96},{1... | collective-permute-start | bytes 393224 | tf_op jit(solution)/shard_map/ppermute | solution.py:15
  87.0 6.2 %all-to-all-done.2 = bf16[8,768,128]{2,1,0:T(8,128)(2,1)S(1)} async-done(((bf16[8,768,128]{2,1,0:T(8,128)(2,1)}), bf16[8,768,128]{2,1,0:T(8,128)(2,1)S(1)}, u32[]{:S(2)}, u32[]{:S(2)}) %all-to-all-start.2) | async-done | bytes 1572896 | tf_op jit(solution)/shard_map/all_to_all | solution.py:285
  93.4 1.0 broadcast_in_dim.31
  94.4 12.5 %all-to-all-start.3 = ((f32[32,2,16,128]{3,1,2,0:T(2,128)}), f32[32,2,16,128]{3,1,2,0:T(2,128)S(1)}, u32[]{:S(2)}, u32[]{:S(2)}) async-start(f32[32,2,16,128]{3,1,2,0:T(2,128)} %bitcast.12), calls=%async_computation.3 | async-start | bytes 1048576 | tf_op jit(solution)/shard_map/all_to_all | solution.py:185
  106.9 0.2 fusion.1
  107.1 0.4 collective-permute-start.13
  107.8 0.2 collective-permute-start.11
  108.0 0.5 collective-permute-done.13
  108.6 0.3 broadcast_select_fusion.3
  108.9 0.3 convert_multiply_fusion.1
  109.3 1.0 copy.21
  110.3 1.2 shard_map.105
  111.5 12.5 %all-to-all-done.3 = f32[32,2,16,128]{3,1,2,0:T(2,128)S(1)} async-done(((f32[32,2,16,128]{3,1,2,0:T(2,128)}), f32[32,2,16,128]{3,1,2,0:T(2,128)S(1)}, u32[]{:S(2)}, u32[]{:S(2)}) %all-to-all-start.3) | async-done | bytes 524320 | tf_op jit(solution)/shard_map/all_to_all | solution.py:185
  124.0 0.3 broadcast_multiply_fusion
  124.4 1.0 copy.22
  (44 shorter events, 0.9 us)
Async XLA Ops:
  0.6 5.9 %collective-permute-start = (bf16[2048,256]{1,0:T(8,128)(2,1)}, bf16[2048,256]{1,0:T(8,128)(2,1)S(1)}, u32[]{:S(2)}, u32[]{:S(2)}) collective-permute-start(bf16[2048,256]{1,0:T(8,128)(2,1)} %refs_2_.1), channel_id=1, source_target_pairs={{0,1},{1,0},{2,3},{3,2},{4,5},{5,4},{6,7},{7,6},{8,9},{9,8},{10,11... | collective-permute-start | bytes 3145736 | tf_op jit(solution)/shard_map/ppermute | solution.py:15
  1.4 25.2 %collective-permute-start.3 = (bf16[2048,256]{1,0:T(8,128)(2,1)}, bf16[2048,256]{1,0:T(8,128)(2,1)}, u32[]{:S(2)}, u32[]{:S(2)}) collective-permute-start(bf16[2048,256]{1,0:T(8,128)(2,1)} %refs_2_.1), channel_id=1, source_target_pairs={{0,16},{16,32},{32,48},{48,64},{64,80},{80,96},{96,112},{112,128},... | collective-permute-start | bytes 3145736 | tf_op jit(solution)/shard_map/ppermute | solution.py:15
  3.0 25.1 %collective-permute-start.4 = (bf16[2048,256]{1,0:T(8,128)(2,1)}, bf16[2048,256]{1,0:T(8,128)(2,1)}, u32[]{:S(2)}, u32[]{:S(2)}) collective-permute-start(bf16[2048,256]{1,0:T(8,128)(2,1)} %refs_2_.1), channel_id=1, source_target_pairs={{0,240},{16,0},{32,16},{48,32},{64,48},{80,64},{96,80},{112,96},{1... | collective-permute-start | bytes 3145736 | tf_op jit(solution)/shard_map/ppermute | solution.py:15
  3.9 2.2 %copy-start = (bf16[2048,256]{1,0:T(8,128)(2,1)S(1)}, bf16[2048,256]{1,0:T(8,128)(2,1)}, u32[]{:S(2)}) copy-start(bf16[2048,256]{1,0:T(8,128)(2,1)} %refs_2_.1) | copy-start | bytes 3145732
  6.6 1.0 copy-start.1
  19.0 36.1 %all-to-all-start = ((bf16[8,1024,128]{2,1,0:T(8,128)(2,1)}), bf16[8,1024,128]{2,1,0:T(8,128)(2,1)}, u32[]{:S(2)}, u32[]{:S(2)}) async-start(bf16[8,1024,128]{2,1,0:T(8,128)(2,1)} %get-tuple-element.20.sides_hbm), calls=%async_computation | async-start | bytes 4194304 | tf_op jit(solution)/shard_map/all_to_all | solution.py:239
  28.2 19.5 %collective-permute-start.5 = (bf16[2048,256]{1,0:T(8,128)(2,1)}, bf16[2048,256]{1,0:T(8,128)(2,1)S(1)}, u32[]{:S(2)}, u32[]{:S(2)}) collective-permute-start(bf16[2048,256]{1,0:T(8,128)(2,1)} %collective-permute-done.3.refs_0_), channel_id=1, source_target_pairs={{0,1},{1,0},{2,3},{3,2},{4,5},{5,4},{6,7},{7,6},{8,9},{9,8},{10,11... | collective-permute-start | bytes 3145736 | tf_op jit(solution)/shard_map/ppermute | solution.py:15
  29.1 18.5 %collective-permute-start.6 = (bf16[2048,256]{1,0:T(8,128)(2,1)}, bf16[2048,256]{1,0:T(8,128)(2,1)S(1)}, u32[]{:S(2)}, u32[]{:S(2)}) collective-permute-start(bf16[2048,256]{1,0:T(8,128)(2,1)} %collective-permute-done.4.refs_4_), channel_id=1, source_target_pairs={{0,1},{1,0},{2,3},{3,2},{4,5},{5,4},{6,7},{7,6},{8,9},{9,8},{10,11... | collective-permute-start | bytes 3145736 | tf_op jit(solution)/shard_map/ppermute | solution.py:15
  29.1 5.1 %collective-permute-start.1 = (f32[2,2,32,128]{3,1,2,0:T(2,128)S(1)}, f32[2,2,32,128]{3,1,2,0:T(2,128)S(1)}, u32[]{:S(2)}, u32[]{:S(2)}) collective-permute-start(f32[2,2,32,128]{3,1,2,0:T(2,128)S(1)} %pad_maximum_fusion.1), channel_id=1, source_target_pairs={{0,16},{16,0},{32,48},{48,32},{64,80},{80,64},{96,112},{112,96},{1... | collective-permute-start | bytes 196616 | tf_op jit(solution)/shard_map/ppermute | solution.py:172
  34.3 5.7 %collective-permute-start.2 = (f32[2,2,32,128]{3,1,2,0:T(2,128)S(1)}, f32[2,2,32,128]{3,1,2,0:T(2,128)S(1)}, u32[]{:S(2)}, u32[]{:S(2)}) collective-permute-start(f32[2,2,32,128]{3,1,2,0:T(2,128)S(1)} %add.56), channel_id=1, source_target_pairs={{0,32},{16,48},{32,0},{48,16},{64,96},{80,112},{96,64},{112,80},{1... | collective-permute-start | bytes 196616 | tf_op jit(solution)/shard_map/ppermute | solution.py:172
  40.1 7.5 %collective-permute-start.7 = (f32[2,2,32,128]{3,1,2,0:T(2,128)S(1)}, f32[2,2,32,128]{3,1,2,0:T(2,128)S(1)}, u32[]{:S(2)}, u32[]{:S(2)}) collective-permute-start(f32[2,2,32,128]{3,1,2,0:T(2,128)S(1)} %add.57), channel_id=1, source_target_pairs={{0,64},{16,80},{32,96},{48,112},{64,0},{80,16},{96,32},{112,48},{1... | collective-permute-start | bytes 196616 | tf_op jit(solution)/shard_map/ppermute | solution.py:172
  47.7 1.1 copy-start.3
  48.7 1.2 copy-start.2
  55.1 14.4 %all-to-all-start.1 = ((bf16[16,64,128]{2,1,0:T(8,128)(2,1)}), bf16[16,64,128]{2,1,0:T(8,128)(2,1)S(1)}, u32[]{:S(2)}, u32[]{:S(2)}) async-start(bf16[16,64,128]{2,1,0:T(8,128)(2,1)} %shard_map.104), calls=%async_computation.1 | async-start | bytes 524288 | tf_op jit(solution)/shard_map/all_to_all | solution.py:270
  61.3 3.2 %collective-permute-start.8 = (f32[2,2,32,128]{3,1,2,0:T(2,128)S(1)}, f32[2,2,32,128]{3,1,2,0:T(2,128)S(1)}, u32[]{:S(2)}, u32[]{:S(2)}) collective-permute-start(f32[2,2,32,128]{3,1,2,0:T(2,128)S(1)} %add.63), channel_id=1, source_target_pairs={{0,128},{16,144},{32,160},{48,176},{64,192},{80,208},{96,224},{112... | collective-permute-start | bytes 196616 | tf_op jit(solution)/shard_map/ppermute | solution.py:172
  70.9 11.2 %copy-start.5 = (bf16[256,512]{1,0:T(8,128)(2,1)S(1)}, bf16[256,512]{1,0:T(8,128)(2,1)}, u32[]{:S(2)}) copy-start(bf16[256,512]{1,0:T(8,128)(2,1)} %param.14) | copy-start | bytes 786436
  70.9 11.4 %copy-start.4 = (bf16[256,512]{1,0:T(8,128)(2,1)S(1)}, bf16[256,512]{1,0:T(8,128)(2,1)}, u32[]{:S(2)}) copy-start(bf16[256,512]{1,0:T(8,128)(2,1)} %param.15) | copy-start | bytes 786436
  70.9 22.4 %all-to-all-start.2 = ((bf16[8,768,128]{2,1,0:T(8,128)(2,1)}), bf16[8,768,128]{2,1,0:T(8,128)(2,1)S(1)}, u32[]{:S(2)}, u32[]{:S(2)}) async-start(bf16[8,768,128]{2,1,0:T(8,128)(2,1)} %pad_maximum_fusion), calls=%async_computation.2 | async-start | bytes 3145728 | tf_op jit(solution)/shard_map/all_to_all | solution.py:285
  77.4 5.7 %collective-permute-start.12 = (bf16[256,256]{1,0:T(8,128)(2,1)S(1)}, bf16[256,256]{1,0:T(8,128)(2,1)S(1)}, u32[]{:S(2)}, u32[]{:S(2)}) collective-permute-start(bf16[256,256]{1,0:T(8,128)(2,1)S(1)} %constant_dynamic-slice_fusion), channel_id=1, source_target_pairs={{0,1},{1,0},{2,3},{3,2},{4,5},{5,4},{6,7},{7,6},{8,9},{9,8},{10,11... | collective-permute-start | bytes 393224 | tf_op jit(solution)/shard_map/ppermute | solution.py:15
  85.3 22.4 %collective-permute-start.10 = (bf16[512,128]{1,0:T(8,128)(2,1)S(1)}, bf16[512,128]{1,0:T(8,128)(2,1)S(1)}, u32[]{:S(2)}, u32[]{:S(2)}) collective-permute-start(bf16[512,128]{1,0:T(8,128)(2,1)S(1)} %get-tuple-element.39), channel_id=1, source_target_pairs={{0,16},{16,32},{32,48},{48,64},{64,80},{80,96},{96,112},{112,128},... | collective-permute-start | bytes 393224 | tf_op jit(solution)/shard_map/ppermute | solution.py:15
  85.7 22.1 %collective-permute-start.9 = (bf16[512,128]{1,0:T(8,128)(2,1)S(1)}, bf16[512,128]{1,0:T(8,128)(2,1)S(1)}, u32[]{:S(2)}, u32[]{:S(2)}) collective-permute-start(bf16[512,128]{1,0:T(8,128)(2,1)S(1)} %get-tuple-element.38), channel_id=1, source_target_pairs={{0,240},{16,0},{32,16},{48,32},{64,48},{80,64},{96,80},{112,96},{1... | collective-permute-start | bytes 393224 | tf_op jit(solution)/shard_map/ppermute | solution.py:15
  94.4 29.6 %all-to-all-start.3 = ((f32[32,2,16,128]{3,1,2,0:T(2,128)}), f32[32,2,16,128]{3,1,2,0:T(2,128)S(1)}, u32[]{:S(2)}, u32[]{:S(2)}) async-start(f32[32,2,16,128]{3,1,2,0:T(2,128)} %bitcast.12), calls=%async_computation.3 | async-start | bytes 1048576 | tf_op jit(solution)/shard_map/all_to_all | solution.py:185
  107.1 1.4 %collective-permute-start.13 = (bf16[8,2,32,128]{3,1,2,0:T(2,128)(2,1)S(1)}, bf16[8,2,32,128]{3,1,2,0:T(2,128)(2,1)S(1)}, u32[]{:S(2)}, u32[]{:S(2)}) collective-permute-start(bf16[8,2,32,128]{3,1,2,0:T(2,128)(2,1)S(1)} %fusion.1), channel_id=1, source_target_pairs={{0,1},{1,0},{2,3},{3,2},{4,5},{5,4},{6,7},{7,6},{8,9},{9,8},{10,11... | collective-permute-start | bytes 393224 | tf_op jit(solution)/shard_map/ppermute | solution.py:15
  107.8 2.5 %collective-permute-start.11 = (f32[2,256,128]{2,1,0:T(8,128)S(1)}, f32[2,256,128]{2,1,0:T(8,128)S(1)}, u32[]{:S(2)}, u32[]{:S(2)}) collective-permute-start(f32[2,256,128]{2,1,0:T(8,128)S(1)} %bitcast.42), channel_id=1, source_target_pairs={{0,1},{1,0},{2,3},{3,2},{4,5},{5,4},{6,7},{7,6},{8,9},{9,8},{10,11... | collective-permute-start | bytes 786440 | tf_op jit(solution)/shard_map/ppermute | solution.py:15

commit v4 on v3

--- a/solution.py
+++ b/solution.py
@@ -106,13 +106,16 @@
     rows = width // targets
     chunks = width // size
     for f in range(2):
-        piece = jnp.where(first, products[f], products[1 - f]).astype(BF)
-        for c in range(chunks):
-            at = (f * chunks + c) * rows
-            for t in range(targets):
-                out_ref[t, at : at + rows, :] = piece[
-                    t * rows : (t + 1) * rows, c * size : (c + 1) * size
-                ]
+        value = jnp.where(first, products[f], products[1 - f])
+        hi = value.astype(BF)
+        lo = (value - hi.astype(F32)).astype(BF)
+        for level, piece in enumerate((hi, lo)):
+            for c in range(chunks):
+                at = ((level * 2 + f) * chunks + c) * rows
+                for t in range(targets):
+                    out_ref[t, at : at + rows, :] = piece[
+                        t * rows : (t + 1) * rows, c * size : (c + 1) * size
+                    ]
 
 
 def product(feat_index, own, sides, features, targets):
@@ -121,7 +124,7 @@
     vmem = pl.BlockSpec(memory_space=pltpu.VMEM)
     smem = pl.BlockSpec(memory_space=pltpu.SMEM)
     hbm = pl.BlockSpec(memory_space=pltpu.HBM)
-    depth = 2 * (width // size) * (width // targets)
+    depth = 4 * (width // size) * (width // targets)
     return pl.pallas_call(
         product_kernel,
         in_specs=[smem] + [hbm] * (2 + len(features)),
@@ -276,7 +279,7 @@
     from_upper = shifted(sides_sum[:edge], "row", -1)
     from_lower = shifted(sides_sum[edge:], "row", 1)
 
-    product_sum = products_got.astype(F32).sum(0)
+    product_sum = products_got.astype(F32).sum(0).reshape(2, -1, lanes).sum(0)
     product_hi = lax.reduce_precision(product_sum, 8, 7)
     product_lo = (product_sum - product_hi).astype(BF)
     self_rows = self_sum.astype(BF).reshape(-1, lanes)
@@ -287,7 +290,7 @@
     end = middle + product_sum.shape[0]
     neighbor_piece = (got[:, edge:middle].astype(F32) + got[:, middle:end].astype(F32)).sum(0)
     neighbor_piece = neighbor_piece.reshape(2, chunks, -1, lanes)
-    neighbor_grad = whole(collect(neighbor_piece), scaling)
+    neighbor_grad = whole(collect(neighbor_piece.astype(BF)), scaling)
 
     summed = got[:, :edge].astype(F32).sum(0)
     h_own = summed + from_upper.astype(F32) + from_lower.astype(F32)

time: 126 us -> 125 us (level)
  waiting for transfers between devices: 38.7 us -> 37.3 us
    all_to_all x1, starting transfers between devices: 12.5 us -> 6.31 us  [collect(): return lax.all_to_all(sent, ('feat', 'row'), 0, 0)]
    ppermute x10, starting transfers between devices: 10.5 us -> 15.7 us  [shifted(): lax.ppermute(array, axis, [(i, (i + by) % size) for i in range(size)])]
    all_to_all x1, waiting for transfers between devices: 12.5 us -> 7.37 us  [collect(): return lax.all_to_all(sent, ('feat', 'row'), 0, 0)]
    all_to_all x1, waiting for transfers between devices: 4.91 us -> 8.33 us  [local(): products_got = lax.all_to_all(products, 'row', 0, 0)]
    unnamed x16 -> x18, local copies, waits for them, and re-layouts: 4.78 us -> 5.58 us
  transfers between devices with their start and end apart: 18 -> 18, of which waited for: 11 -> 10; matrix products, arithmetic and copies ran while one was open for 8% -> 8% of each run, Pallas kernels for 14% -> 14%
where the time goes in v4:
time: 125 us; the launch traced here: 123 us
  starting transfers between devices  52.2 us (42%)
  waiting for transfers between devices  37.3 us (30%)
  Pallas kernels  17.2 us (14%)
  other arithmetic  7.81 us (6%)
  local copies, waits for them, and re-layouts  6.7 us (5%)
  matrix products  1.38 us (1%)
    ppermute x10, starting transfers between devices, shifted(): lax.ppermute(array, axis, [(i, (i + by) % size) for i in range(size)])  15.7 us
    pallas_call x1, Pallas kernels, sparse_pass(): pl.pallas_call(sparse_kernel, in_specs=[smem, hbm, vmem], out_specs=[vmem...  11.5 us
    ppermute x4, waiting for transfers between devices, exchanged(): lax.ppermute(value, 'row', [(i, i ^ step) for i in range(count)])  11.4 us
    ppermute x4, starting transfers between devices, exchanged(): lax.ppermute(value, 'row', [(i, i ^ step) for i in range(count)])  10.3 us
    all_to_all x1, waiting for transfers between devices, local(): products_got = lax.all_to_all(products, 'row', 0, 0)  8.33 us
    all_to_all x1, waiting for transfers between devices, collect(): return lax.all_to_all(sent, ('feat', 'row'), 0, 0)  7.37 us
    all_to_all x1, starting transfers between devices, local(): got = lax.all_to_all(jnp.concatenate([own, to_all], axis=1), 'rep', 0, 0)  6.94 us
    all_to_all x1, waiting for transfers between devices, local(): got = lax.all_to_all(jnp.concatenate([own, to_all], axis=1), 'rep', 0, 0)  6.93 us
  transfers between devices with their start and end apart: 18, of which 10 were waited for; matrix products, arithmetic and copies ran while one was open for 8% of the time, Pallas kernels for 14%

profile of v4, /device:TPU:33, one launch (start us, length us, event | category | flops | bytes accessed | tf_op | source)
XLA Modules:
  0.0 123.4 jit_solution(7330760635039956869)
XLA Ops:
  0.6 0.8 collective-permute-start
  1.4 1.7 %collective-permute-start.3 = (bf16[2048,256]{1,0:T(8,128)(2,1)}, bf16[2048,256]{1,0:T(8,128)(2,1)}, u32[]{:S(2)}, u32[]{:S(2)}) collective-permute-start(bf16[2048,256]{1,0:T(8,128)(2,1)} %refs_2_.1), channel_id=1, source_target_pairs={{0,16},{16,32},{32,48},{48,64},{64,80},{80,96},{96,112},{112,128},... | collective-permute-start | bytes 3145736 | tf_op jit(solution)/shard_map/ppermute | solution.py:15
  3.1 0.8 fusion.15
  3.9 2.1 %convert_multiply_fusion.g_ref = bf16[2048,256]{1,0:T(8,128)(2,1)S(1)} fusion(bf16[2048,256]{1,0:T(8,128)(2,1)} %param.9, s32[2048,256]{1,0:T(8,128)} %param.10), kind=kLoop, calls=%fused_computation.4 | loop fusion | flops 1048576 | bytes 4194304 | tf_op jit(solution)/shard_map/mul | solution.py:224
  6.1 0.5 fusion.19
  6.6 0.5 fusion.20
  7.1 0.4 copy-done.1
  7.6 11.5 %shard_map.103 = (bf16[8,1024,128]{2,1,0:T(8,128)(2,1)}, bf16[8,512,128]{2,1,0:T(8,128)(2,1)S(1)}) custom-call(s32[256]{0:T(256)S(1)} %reshape.56.pos_ref, bf16[16,16,128,128]{3,2,1,0:T(8,128)(2,1)} %w_hbm.1, bf16[2048,256]{1,0:T(8,128)(2,1)S(1)} %convert_multiply_fusion.g_ref), custom_call_target="tpu_custom_call" | custom-call | flops 2147483648 | bytes 13631488 | tf_op jit(solution)/shard_map/pallas_call | solution.py:56
  19.1 6.7 %all-to-all-start = ((bf16[8,1024,128]{2,1,0:T(8,128)(2,1)}), bf16[8,1024,128]{2,1,0:T(8,128)(2,1)}, u32[]{:S(2)}, u32[]{:S(2)}) async-start(bf16[8,1024,128]{2,1,0:T(8,128)(2,1)} %get-tuple-element.20.sides_hbm), calls=%async_computation | async-start | bytes 4194304 | tf_op jit(solution)/shard_map/all_to_all | solution.py:242
  25.7 0.9 collective-permute-done.3.refs_0_
  26.6 1.6 %collective-permute-done.4.refs_4_ = bf16[2048,256]{1,0:T(8,128)(2,1)} collective-permute-done((bf16[2048,256]{1,0:T(8,128)(2,1)}, bf16[2048,256]{1,0:T(8,128)(2,1)}, u32[]{:S(2)}, u32[]{:S(2)}) %collective-permute-start.4) | collective-permute-done | bytes 1048608 | tf_op jit(solution)/shard_map/ppermute | solution.py:15
  28.2 1.0 collective-permute-start.5
  29.1 3.0 %collective-permute-start.1 = (f32[2,2,32,128]{3,1,2,0:T(2,128)S(1)}, f32[2,2,32,128]{3,1,2,0:T(2,128)S(1)}, u32[]{:S(2)}, u32[]{:S(2)}) collective-permute-start(f32[2,2,32,128]{3,1,2,0:T(2,128)S(1)} %pad_maximum_fusion.1), channel_id=1, source_target_pairs={{0,16},{16,0},{32,48},{48,32},{64,80},{80,64},{96,112},{112,96},{1... | collective-permute-start | bytes 196616 | tf_op jit(solution)/shard_map/ppermute | solution.py:175
  32.2 2.1 %collective-permute-done.1 = f32[2,2,32,128]{3,1,2,0:T(2,128)S(1)} collective-permute-done((f32[2,2,32,128]{3,1,2,0:T(2,128)S(1)}, f32[2,2,32,128]{3,1,2,0:T(2,128)S(1)}, u32[]{:S(2)}, u32[]{:S(2)}) %collective-permute-start.1) | collective-permute-done | bytes 65568 | tf_op jit(solution)/shard_map/ppermute | solution.py:175
  34.3 3.7 %collective-permute-start.2 = (f32[2,2,32,128]{3,1,2,0:T(2,128)S(1)}, f32[2,2,32,128]{3,1,2,0:T(2,128)S(1)}, u32[]{:S(2)}, u32[]{:S(2)}) collective-permute-start(f32[2,2,32,128]{3,1,2,0:T(2,128)S(1)} %add.56), channel_id=1, source_target_pairs={{0,32},{16,48},{32,0},{48,16},{64,96},{80,112},{96,64},{112,80},{1... | collective-permute-start | bytes 196616 | tf_op jit(solution)/shard_map/ppermute | solution.py:175
  38.0 2.1 %collective-permute-done.2 = f32[2,2,32,128]{3,1,2,0:T(2,128)S(1)} collective-permute-done((f32[2,2,32,128]{3,1,2,0:T(2,128)S(1)}, f32[2,2,32,128]{3,1,2,0:T(2,128)S(1)}, u32[]{:S(2)}, u32[]{:S(2)}) %collective-permute-start.2) | collective-permute-done | bytes 65568 | tf_op jit(solution)/shard_map/ppermute | solution.py:175
  40.1 2.4 %collective-permute-start.7 = (f32[2,2,32,128]{3,1,2,0:T(2,128)S(1)}, f32[2,2,32,128]{3,1,2,0:T(2,128)S(1)}, u32[]{:S(2)}, u32[]{:S(2)}) collective-permute-start(f32[2,2,32,128]{3,1,2,0:T(2,128)S(1)} %add.57), channel_id=1, source_target_pairs={{0,64},{16,80},{32,96},{48,112},{64,0},{80,16},{96,32},{112,48},{1... | collective-permute-start | bytes 196616 | tf_op jit(solution)/shard_map/ppermute | solution.py:175
  42.5 5.1 %collective-permute-done.7 = f32[2,2,32,128]{3,1,2,0:T(2,128)S(1)} collective-permute-done((f32[2,2,32,128]{3,1,2,0:T(2,128)S(1)}, f32[2,2,32,128]{3,1,2,0:T(2,128)S(1)}, u32[]{:S(2)}, u32[]{:S(2)}) %collective-permute-start.7) | collective-permute-done | bytes 65568 | tf_op jit(solution)/shard_map/ppermute | solution.py:175
  47.7 1.0 copy-done.4
  48.7 1.2 copy-done.2
  49.9 4.5 %shard_map.104 = bf16[16,128,128]{2,1,0:T(8,128)(2,1)S(1)} custom-call(s32[1]{0:T(128)} %bitcast.4.feat_ref, bf16[8,512,128]{2,1,0:T(8,128)(2,1)S(1)} %get-tuple-element.19.own_hbm, bf16[8,1024,128]{2,1,0:T(8,128)(2,1)} %get-tuple-element.20.sides_hbm, bf16[2048,256]{1,0:T(8,128)(2,1)} %collective-permute-done.3.refs_0_, ...), custom_call_target="tpu_custom_call" | custom-call | flops 1610612736 | bytes 10485760 | tf_op jit(solution)/shard_map/pallas_call | solution.py:128
  54.4 0.8 copy-done.3
  55.2 6.2 %all-to-all-start.1 = ((bf16[16,128,128]{2,1,0:T(8,128)(2,1)}), bf16[16,128,128]{2,1,0:T(8,128)(2,1)S(1)}, u32[]{:S(2)}, u32[]{:S(2)}) async-start(bf16[16,128,128]{2,1,0:T(8,128)(2,1)} %copy-done.3), calls=%async_computation.1 | async-start | bytes 1048576 | tf_op jit(solution)/shard_map/all_to_all | solution.py:273
  61.4 1.2 collective-permute-start.8
  62.6 2.2 %collective-permute-done.8 = f32[2,2,32,128]{3,1,2,0:T(2,128)S(1)} collective-permute-done((f32[2,2,32,128]{3,1,2,0:T(2,128)S(1)}, f32[2,2,32,128]{3,1,2,0:T(2,128)S(1)}, u32[]{:S(2)}, u32[]{:S(2)}) %collective-permute-start.8) | collective-permute-done | bytes 65568 | tf_op jit(solution)/shard_map/ppermute | solution.py:175
  64.8 8.3 %all-to-all-done.1 = bf16[16,128,128]{2,1,0:T(8,128)(2,1)S(1)} async-done(((bf16[16,128,128]{2,1,0:T(8,128)(2,1)}), bf16[16,128,128]{2,1,0:T(8,128)(2,1)S(1)}, u32[]{:S(2)}, u32[]{:S(2)}) %all-to-all-start.1) | async-done | bytes 524320 | tf_op jit(solution)/shard_map/all_to_all | solution.py:273
  73.4 1.2 %pad_maximum_fusion = bf16[8,768,128]{2,1,0:T(8,128)(2,1)} fusion(bf16[8,256,128]{2,1,0:T(8,128)(2,1)S(1)} %broadcast_in_dim.28, bf16[8,512,128]{2,1,0:T(8,128)(2,1)S(1)} %get-tuple-element.19.own_hbm), kind=kLoop, calls=%fused_computation.1 | loop fusion | flops 3145728 | bytes 3145728 | tf_op jit(solution)/shard_map/concatenate | solution.py:288
  74.6 6.9 %all-to-all-start.2 = ((bf16[8,768,128]{2,1,0:T(8,128)(2,1)}), bf16[8,768,128]{2,1,0:T(8,128)(2,1)S(1)}, u32[]{:S(2)}, u32[]{:S(2)}) async-start(bf16[8,768,128]{2,1,0:T(8,128)(2,1)} %pad_maximum_fusion), calls=%async_computation.2 | async-start | bytes 3145728 | tf_op jit(solution)/shard_map/all_to_all | solution.py:288
  81.6 4.5 %collective-permute-start.12 = (bf16[256,256]{1,0:T(8,128)(2,1)S(1)}, bf16[256,256]{1,0:T(8,128)(2,1)S(1)}, u32[]{:S(2)}, u32[]{:S(2)}) collective-permute-start(bf16[256,256]{1,0:T(8,128)(2,1)S(1)} %constant_dynamic-slice_fusion), channel_id=1, source_target_pairs={{0,1},{1,0},{2,3},{3,2},{4,5},{5,4},{6,7},{7,6},{8,9},{9,8},{10,11... | collective-permute-start | bytes 393224 | tf_op jit(solution)/shard_map/ppermute | solution.py:15
  86.0 0.2 fusion.3
  86.3 0.7 collective-permute-done.12
  87.0 0.2 convolution_add_fusion.self_ref
  87.3 2.0 %reduce_sum.51 = bf16[1024,128]{1,0:T(8,128)(2,1)S(1)} reduce(bf16[8,1024,128]{2,1,0:T(8,128)(2,1)} %all-to-all-done, bf16[]{:T(256)} %constant.65.clone.1), dimensions={0}, to_apply=%region_3.4 | reduce | flops 917504 | bytes 2359298 | tf_op jit(solution)/shard_map/reduce_sum | solution.py:278
  89.3 0.9 collective-permute-start.10
  90.2 0.8 collective-permute-start.9
  91.0 6.9 %all-to-all-done.2 = bf16[8,768,128]{2,1,0:T(8,128)(2,1)S(1)} async-done(((bf16[8,768,128]{2,1,0:T(8,128)(2,1)}), bf16[8,768,128]{2,1,0:T(8,128)(2,1)S(1)}, u32[]{:S(2)}, u32[]{:S(2)}) %all-to-all-start.2) | async-done | bytes 1572896 | tf_op jit(solution)/shard_map/all_to_all | solution.py:288
  98.0 0.2 fusion.1
  98.2 5.7 %collective-permute-start.13 = (bf16[8,2,32,128]{3,1,2,0:T(2,128)(2,1)S(1)}, bf16[8,2,32,128]{3,1,2,0:T(2,128)(2,1)S(1)}, u32[]{:S(2)}, u32[]{:S(2)}) collective-permute-start(bf16[8,2,32,128]{3,1,2,0:T(2,128)(2,1)S(1)} %fusion.1), channel_id=1, source_target_pairs={{0,1},{1,0},{2,3},{3,2},{4,5},{5,4},{6,7},{7,6},{8,9},{9,8},{10,11... | collective-permute-start | bytes 393224 | tf_op jit(solution)/shard_map/ppermute | solution.py:15
  104.0 0.8 broadcast_in_dim.29
  104.8 6.3 %all-to-all-start.3 = ((bf16[32,2,16,128]{3,1,2,0:T(2,128)(2,1)}), bf16[32,2,16,128]{3,1,2,0:T(2,128)(2,1)S(1)}, u32[]{:S(2)}, u32[]{:S(2)}) async-start(bf16[32,2,16,128]{3,1,2,0:T(2,128)(2,1)} %bitcast.13), calls=%async_computation.3 | async-start | bytes 524288 | tf_op jit(solution)/shard_map/all_to_all | solution.py:188
  111.3 0.4 collective-permute-start.11
  111.8 0.3 broadcast_select_fusion.3
  112.1 0.3 convert_multiply_fusion.2
  112.5 1.0 copy.27
  113.5 1.2 shard_map.105
  114.7 7.4 %all-to-all-done.3 = bf16[32,2,16,128]{3,1,2,0:T(2,128)(2,1)S(1)} async-done(((bf16[32,2,16,128]{3,1,2,0:T(2,128)(2,1)}), bf16[32,2,16,128]{3,1,2,0:T(2,128)(2,1)S(1)}, u32[]{:S(2)}, u32[]{:S(2)}) %all-to-all-start.3) | async-done | bytes 262176 | tf_op jit(solution)/shard_map/all_to_all | solution.py:188
  122.1 0.3 convert_multiply_fusion.1
  122.4 1.0 copy.28
  (47 shorter events, 1.0 us)
Async XLA Ops:
  0.6 5.9 %collective-permute-start = (bf16[2048,256]{1,0:T(8,128)(2,1)}, bf16[2048,256]{1,0:T(8,128)(2,1)S(1)}, u32[]{:S(2)}, u32[]{:S(2)}) collective-permute-start(bf16[2048,256]{1,0:T(8,128)(2,1)} %refs_2_.1), channel_id=1, source_target_pairs={{0,1},{1,0},{2,3},{3,2},{4,5},{5,4},{6,7},{7,6},{8,9},{9,8},{10,11... | collective-permute-start | bytes 3145736 | tf_op jit(solution)/shard_map/ppermute | solution.py:15
  1.4 25.2 %collective-permute-start.3 = (bf16[2048,256]{1,0:T(8,128)(2,1)}, bf16[2048,256]{1,0:T(8,128)(2,1)}, u32[]{:S(2)}, u32[]{:S(2)}) collective-permute-start(bf16[2048,256]{1,0:T(8,128)(2,1)} %refs_2_.1), channel_id=1, source_target_pairs={{0,16},{16,32},{32,48},{48,64},{64,80},{80,96},{96,112},{112,128},... | collective-permute-start | bytes 3145736 | tf_op jit(solution)/shard_map/ppermute | solution.py:15
  3.0 25.1 %collective-permute-start.4 = (bf16[2048,256]{1,0:T(8,128)(2,1)}, bf16[2048,256]{1,0:T(8,128)(2,1)}, u32[]{:S(2)}, u32[]{:S(2)}) collective-permute-start(bf16[2048,256]{1,0:T(8,128)(2,1)} %refs_2_.1), channel_id=1, source_target_pairs={{0,240},{16,0},{32,16},{48,32},{64,48},{80,64},{96,80},{112,96},{1... | collective-permute-start | bytes 3145736 | tf_op jit(solution)/shard_map/ppermute | solution.py:15
  3.9 2.2 %copy-start = (bf16[2048,256]{1,0:T(8,128)(2,1)S(1)}, bf16[2048,256]{1,0:T(8,128)(2,1)}, u32[]{:S(2)}) copy-start(bf16[2048,256]{1,0:T(8,128)(2,1)} %refs_2_.1) | copy-start | bytes 3145732
  6.6 1.0 copy-start.1
  19.1 36.1 %all-to-all-start = ((bf16[8,1024,128]{2,1,0:T(8,128)(2,1)}), bf16[8,1024,128]{2,1,0:T(8,128)(2,1)}, u32[]{:S(2)}, u32[]{:S(2)}) async-start(bf16[8,1024,128]{2,1,0:T(8,128)(2,1)} %get-tuple-element.20.sides_hbm), calls=%async_computation | async-start | bytes 4194304 | tf_op jit(solution)/shard_map/all_to_all | solution.py:242
  28.2 19.5 %collective-permute-start.5 = (bf16[2048,256]{1,0:T(8,128)(2,1)}, bf16[2048,256]{1,0:T(8,128)(2,1)S(1)}, u32[]{:S(2)}, u32[]{:S(2)}) collective-permute-start(bf16[2048,256]{1,0:T(8,128)(2,1)} %collective-permute-done.3.refs_0_), channel_id=1, source_target_pairs={{0,1},{1,0},{2,3},{3,2},{4,5},{5,4},{6,7},{7,6},{8,9},{9,8},{10,11... | collective-permute-start | bytes 3145736 | tf_op jit(solution)/shard_map/ppermute | solution.py:15
  29.1 18.5 %collective-permute-start.6 = (bf16[2048,256]{1,0:T(8,128)(2,1)}, bf16[2048,256]{1,0:T(8,128)(2,1)S(1)}, u32[]{:S(2)}, u32[]{:S(2)}) collective-permute-start(bf16[2048,256]{1,0:T(8,128)(2,1)} %collective-permute-done.4.refs_4_), channel_id=1, source_target_pairs={{0,1},{1,0},{2,3},{3,2},{4,5},{5,4},{6,7},{7,6},{8,9},{9,8},{10,11... | collective-permute-start | bytes 3145736 | tf_op jit(solution)/shard_map/ppermute | solution.py:15
  29.1 5.1 %collective-permute-start.1 = (f32[2,2,32,128]{3,1,2,0:T(2,128)S(1)}, f32[2,2,32,128]{3,1,2,0:T(2,128)S(1)}, u32[]{:S(2)}, u32[]{:S(2)}) collective-permute-start(f32[2,2,32,128]{3,1,2,0:T(2,128)S(1)} %pad_maximum_fusion.1), channel_id=1, source_target_pairs={{0,16},{16,0},{32,48},{48,32},{64,80},{80,64},{96,112},{112,96},{1... | collective-permute-start | bytes 196616 | tf_op jit(solution)/shard_map/ppermute | solution.py:175
  34.3 5.7 %collective-permute-start.2 = (f32[2,2,32,128]{3,1,2,0:T(2,128)S(1)}, f32[2,2,32,128]{3,1,2,0:T(2,128)S(1)}, u32[]{:S(2)}, u32[]{:S(2)}) collective-permute-start(f32[2,2,32,128]{3,1,2,0:T(2,128)S(1)} %add.56), channel_id=1, source_target_pairs={{0,32},{16,48},{32,0},{48,16},{64,96},{80,112},{96,64},{112,80},{1... | collective-permute-start | bytes 196616 | tf_op jit(solution)/shard_map/ppermute | solution.py:175
  40.1 7.5 %collective-permute-start.7 = (f32[2,2,32,128]{3,1,2,0:T(2,128)S(1)}, f32[2,2,32,128]{3,1,2,0:T(2,128)S(1)}, u32[]{:S(2)}, u32[]{:S(2)}) collective-permute-start(f32[2,2,32,128]{3,1,2,0:T(2,128)S(1)} %add.57), channel_id=1, source_target_pairs={{0,64},{16,80},{32,96},{48,112},{64,0},{80,16},{96,32},{112,48},{1... | collective-permute-start | bytes 196616 | tf_op jit(solution)/shard_map/ppermute | solution.py:175
  47.7 1.1 copy-start.4
  48.7 1.2 copy-start.2
  54.4 0.8 copy-start.3
  55.2 18.0 %all-to-all-start.1 = ((bf16[16,128,128]{2,1,0:T(8,128)(2,1)}), bf16[16,128,128]{2,1,0:T(8,128)(2,1)S(1)}, u32[]{:S(2)}, u32[]{:S(2)}) async-start(bf16[16,128,128]{2,1,0:T(8,128)(2,1)} %copy-done.3), calls=%async_computation.1 | async-start | bytes 1048576 | tf_op jit(solution)/shard_map/all_to_all | solution.py:273
  61.4 3.4 %collective-permute-start.8 = (f32[2,2,32,128]{3,1,2,0:T(2,128)S(1)}, f32[2,2,32,128]{3,1,2,0:T(2,128)S(1)}, u32[]{:S(2)}, u32[]{:S(2)}) collective-permute-start(f32[2,2,32,128]{3,1,2,0:T(2,128)S(1)} %add.63), channel_id=1, source_target_pairs={{0,128},{16,144},{32,160},{48,176},{64,192},{80,208},{96,224},{112... | collective-permute-start | bytes 196616 | tf_op jit(solution)/shard_map/ppermute | solution.py:175
  74.6 11.4 %copy-start.6 = (bf16[256,512]{1,0:T(8,128)(2,1)S(1)}, bf16[256,512]{1,0:T(8,128)(2,1)}, u32[]{:S(2)}) copy-start(bf16[256,512]{1,0:T(8,128)(2,1)} %param.14) | copy-start | bytes 786436
  74.6 11.7 %copy-start.5 = (bf16[256,512]{1,0:T(8,128)(2,1)S(1)}, bf16[256,512]{1,0:T(8,128)(2,1)}, u32[]{:S(2)}) copy-start(bf16[256,512]{1,0:T(8,128)(2,1)} %param.15) | copy-start | bytes 786436
  74.6 23.3 %all-to-all-start.2 = ((bf16[8,768,128]{2,1,0:T(8,128)(2,1)}), bf16[8,768,128]{2,1,0:T(8,128)(2,1)S(1)}, u32[]{:S(2)}, u32[]{:S(2)}) async-start(bf16[8,768,128]{2,1,0:T(8,128)(2,1)} %pad_maximum_fusion), calls=%async_computation.2 | async-start | bytes 3145728 | tf_op jit(solution)/shard_map/all_to_all | solution.py:288
  81.6 5.5 %collective-permute-start.12 = (bf16[256,256]{1,0:T(8,128)(2,1)S(1)}, bf16[256,256]{1,0:T(8,128)(2,1)S(1)}, u32[]{:S(2)}, u32[]{:S(2)}) collective-permute-start(bf16[256,256]{1,0:T(8,128)(2,1)S(1)} %constant_dynamic-slice_fusion), channel_id=1, source_target_pairs={{0,1},{1,0},{2,3},{3,2},{4,5},{5,4},{6,7},{7,6},{8,9},{9,8},{10,11... | collective-permute-start | bytes 393224 | tf_op jit(solution)/shard_map/ppermute | solution.py:15
  89.3 22.0 %collective-permute-start.10 = (bf16[512,128]{1,0:T(8,128)(2,1)S(1)}, bf16[512,128]{1,0:T(8,128)(2,1)S(1)}, u32[]{:S(2)}, u32[]{:S(2)}) collective-permute-start(bf16[512,128]{1,0:T(8,128)(2,1)S(1)} %get-tuple-element.42), channel_id=1, source_target_pairs={{0,16},{16,32},{32,48},{48,64},{64,80},{80,96},{96,112},{112,128},... | collective-permute-start | bytes 393224 | tf_op jit(solution)/shard_map/ppermute | solution.py:15
  90.2 21.1 %collective-permute-start.9 = (bf16[512,128]{1,0:T(8,128)(2,1)S(1)}, bf16[512,128]{1,0:T(8,128)(2,1)S(1)}, u32[]{:S(2)}, u32[]{:S(2)}) collective-permute-start(bf16[512,128]{1,0:T(8,128)(2,1)S(1)} %get-tuple-element.41), channel_id=1, source_target_pairs={{0,240},{16,0},{32,16},{48,32},{64,48},{80,64},{96,80},{112,96},{1... | collective-permute-start | bytes 393224 | tf_op jit(solution)/shard_map/ppermute | solution.py:15
  98.2 13.6 %collective-permute-start.13 = (bf16[8,2,32,128]{3,1,2,0:T(2,128)(2,1)S(1)}, bf16[8,2,32,128]{3,1,2,0:T(2,128)(2,1)S(1)}, u32[]{:S(2)}, u32[]{:S(2)}) collective-permute-start(bf16[8,2,32,128]{3,1,2,0:T(2,128)(2,1)S(1)} %fusion.1), channel_id=1, source_target_pairs={{0,1},{1,0},{2,3},{3,2},{4,5},{5,4},{6,7},{7,6},{8,9},{9,8},{10,11... | collective-permute-start | bytes 393224 | tf_op jit(solution)/shard_map/ppermute | solution.py:15
  104.8 17.3 %all-to-all-start.3 = ((bf16[32,2,16,128]{3,1,2,0:T(2,128)(2,1)}), bf16[32,2,16,128]{3,1,2,0:T(2,128)(2,1)S(1)}, u32[]{:S(2)}, u32[]{:S(2)}) async-start(bf16[32,2,16,128]{3,1,2,0:T(2,128)(2,1)} %bitcast.13), calls=%async_computation.3 | async-start | bytes 524288 | tf_op jit(solution)/shard_map/all_to_all | solution.py:188
  111.3 2.2 %collective-permute-start.11 = (f32[2,256,128]{2,1,0:T(8,128)S(1)}, f32[2,256,128]{2,1,0:T(8,128)S(1)}, u32[]{:S(2)}, u32[]{:S(2)}) collective-permute-start(f32[2,256,128]{2,1,0:T(8,128)S(1)} %bitcast.43), channel_id=1, source_target_pairs={{0,1},{1,0},{2,3},{3,2},{4,5},{5,4},{6,7},{7,6},{8,9},{9,8},{10,11... | collective-permute-start | bytes 786440 | tf_op jit(solution)/shard_map/ppermute | solution.py:15

commit v5 on v4

--- a/solution.py
+++ b/solution.py
@@ -237,10 +237,9 @@
     self_piece = jnp.stack(
         [jnp.where(first, self_own, self_oth), jnp.where(first, self_oth, self_own)]
     )
-    self_piece, grad_values = lax.optimization_barrier((self_piece, masked_grad))
-    sides, own = sparse_pass(destinations, block_weights, grad_values, rep_devices)
+    sides, own = sparse_pass(destinations, block_weights, masked_grad, rep_devices)
     sides_got = lax.all_to_all(sides, "rep", 0, 0)
-    before, after, own = lax.optimization_barrier((before, after, own))
+    before, after, own, self_piece = lax.optimization_barrier((before, after, own, self_piece))
     self_sum, step = self_piece, 1
     while 4 * step < row_devices:
         self_sum = exchanged(self_sum, step)

time: 125 us -> 124 us (level)
  waiting for transfers between devices: 37.3 us -> 34.6 us
    all_to_all x1, waiting for transfers between devices: 6.93 us -> 5.19 us  [local(): got = lax.all_to_all(jnp.concatenate([own, to_all], axis=1), 'rep', 0, 0)]
    unnamed x18, local copies, waits for them, and re-layouts: 5.58 us -> 3.92 us
  transfers between devices with their start and end apart: 18 -> 18, of which waited for: 10 -> 10; matrix products, arithmetic and copies ran while one was open for 8% -> 10% of each run, Pallas kernels for 14% -> 14%
where the time goes in v5:
time: 124 us; the launch traced here: 122 us
  starting transfers between devices  53.2 us (43%)
  waiting for transfers between devices  34.6 us (28%)
  Pallas kernels  17.5 us (14%)
  other arithmetic  8.01 us (6%)
  local copies, waits for them, and re-layouts  5.7 us (5%)
  matrix products  2.6 us (2%)
    ppermute x10, starting transfers between devices, shifted(): lax.ppermute(array, axis, [(i, (i + by) % size) for i in range(size)])  16.8 us
    pallas_call x1, Pallas kernels, sparse_pass(): pl.pallas_call(sparse_kernel, in_specs=[smem, hbm, vmem], out_specs=[vmem...  11.5 us
    ppermute x4, waiting for transfers between devices, exchanged(): lax.ppermute(value, 'row', [(i, i ^ step) for i in range(count)])  11.4 us
    ppermute x4, starting transfers between devices, exchanged(): lax.ppermute(value, 'row', [(i, i ^ step) for i in range(count)])  10.3 us
    all_to_all x1, waiting for transfers between devices, local(): products_got = lax.all_to_all(products, 'row', 0, 0)  8.55 us
    all_to_all x1, starting transfers between devices, collect(): return lax.all_to_all(sent, ('feat', 'row'), 0, 0)  6.85 us
    all_to_all x1, starting transfers between devices, local(): sides_got = lax.all_to_all(sides, 'rep', 0, 0)  6.8 us
    all_to_all x1, starting transfers between devices, local(): products_got = lax.all_to_all(products, 'row', 0, 0)  6.43 us
  transfers between devices with their start and end apart: 18, of which 10 were waited for; matrix products, arithmetic and copies ran while one was open for 10% of the time, Pallas kernels for 14%

profile of v5, /device:TPU:33, one launch (start us, length us, event | category | flops | bytes accessed | tf_op | source)
XLA Modules:
  0.0 122.5 jit_solution(16693262137676472511)
XLA Ops:
  0.6 0.8 collective-permute-start.2
  1.4 1.7 %collective-permute-start = (bf16[2048,256]{1,0:T(8,128)(2,1)}, bf16[2048,256]{1,0:T(8,128)(2,1)}, u32[]{:S(2)}, u32[]{:S(2)}) collective-permute-start(bf16[2048,256]{1,0:T(8,128)(2,1)} %refs_2_.1), channel_id=1, source_target_pairs={{0,16},{16,32},{32,48},{48,64},{64,80},{80,96},{96,112},{112,128},... | collective-permute-start | bytes 3145736 | tf_op jit(solution)/shard_map/ppermute | solution.py:15
  3.1 2.1 %convert_multiply_fusion.g_ref = bf16[2048,256]{1,0:T(8,128)(2,1)S(1)} fusion(bf16[2048,256]{1,0:T(8,128)(2,1)} %param.9, s32[2048,256]{1,0:T(8,128)} %param.10), kind=kLoop, calls=%fused_computation.4 | loop fusion | flops 1048576 | bytes 4194304 | tf_op jit(solution)/shard_map/mul | solution.py:224
  5.3 11.5 %shard_map.103 = (bf16[8,1024,128]{2,1,0:T(8,128)(2,1)}, bf16[8,512,128]{2,1,0:T(8,128)(2,1)S(1)}) custom-call(s32[256]{0:T(256)S(1)} %reshape.56.pos_ref, bf16[16,16,128,128]{3,2,1,0:T(8,128)(2,1)} %w_hbm.1, bf16[2048,256]{1,0:T(8,128)(2,1)S(1)} %convert_multiply_fusion.g_ref), custom_call_target="tpu_custom_call" | custom-call | flops 2147483648 | bytes 13631488 | tf_op jit(solution)/shard_map/pallas_call | solution.py:56
  16.8 6.8 %all-to-all-start = ((bf16[8,1024,128]{2,1,0:T(8,128)(2,1)}), bf16[8,1024,128]{2,1,0:T(8,128)(2,1)}, u32[]{:S(2)}, u32[]{:S(2)}) async-start(bf16[8,1024,128]{2,1,0:T(8,128)(2,1)} %get-tuple-element.18.sides_hbm), calls=%async_computation | async-start | bytes 4194304 | tf_op jit(solution)/shard_map/all_to_all | solution.py:241
  23.6 0.5 fusion.19
  24.1 1.7 %fusion.20 = f32[256,256]{1,0:T(8,128)S(1)} fusion(bf16[2048,256]{1,0:T(8,128)(2,1)S(1)} %convert_multiply_fusion.g_ref, bf16[2048,256]{1,0:T(8,128)(2,1)} %collective-permute-done.2.refs_3_), kind=kOutput, calls=%fused_computation.55 | convolution fusion | flops 268435456 | bytes 2359296 | tf_op jit(solution)/shard_map/ro,rd->od/dot_general | solution.py:231
  25.9 0.7 collective-permute-done.refs_0_
  26.6 1.6 %collective-permute-done.1.refs_4_ = bf16[2048,256]{1,0:T(8,128)(2,1)} collective-permute-done((bf16[2048,256]{1,0:T(8,128)(2,1)}, bf16[2048,256]{1,0:T(8,128)(2,1)}, u32[]{:S(2)}, u32[]{:S(2)}) %collective-permute-start.1) | collective-permute-done | bytes 1048608 | tf_op jit(solution)/shard_map/ppermute | solution.py:15
  28.2 1.0 collective-permute-start.5
  29.1 3.1 %collective-permute-start.3 = (f32[2,2,32,128]{3,1,2,0:T(2,128)S(1)}, f32[2,2,32,128]{3,1,2,0:T(2,128)S(1)}, u32[]{:S(2)}, u32[]{:S(2)}) collective-permute-start(f32[2,2,32,128]{3,1,2,0:T(2,128)S(1)} %pad_maximum_fusion.1), channel_id=1, source_target_pairs={{0,16},{16,0},{32,48},{48,32},{64,80},{80,64},{96,112},{112,96},{1... | collective-permute-start | bytes 196616 | tf_op jit(solution)/shard_map/ppermute | solution.py:175
  32.3 2.1 %collective-permute-done.3 = f32[2,2,32,128]{3,1,2,0:T(2,128)S(1)} collective-permute-done((f32[2,2,32,128]{3,1,2,0:T(2,128)S(1)}, f32[2,2,32,128]{3,1,2,0:T(2,128)S(1)}, u32[]{:S(2)}, u32[]{:S(2)}) %collective-permute-start.3) | collective-permute-done | bytes 65568 | tf_op jit(solution)/shard_map/ppermute | solution.py:175
  34.4 3.6 %collective-permute-start.4 = (f32[2,2,32,128]{3,1,2,0:T(2,128)S(1)}, f32[2,2,32,128]{3,1,2,0:T(2,128)S(1)}, u32[]{:S(2)}, u32[]{:S(2)}) collective-permute-start(f32[2,2,32,128]{3,1,2,0:T(2,128)S(1)} %add.61), channel_id=1, source_target_pairs={{0,32},{16,48},{32,0},{48,16},{64,96},{80,112},{96,64},{112,80},{1... | collective-permute-start | bytes 196616 | tf_op jit(solution)/shard_map/ppermute | solution.py:175
  38.0 2.1 %collective-permute-done.4 = f32[2,2,32,128]{3,1,2,0:T(2,128)S(1)} collective-permute-done((f32[2,2,32,128]{3,1,2,0:T(2,128)S(1)}, f32[2,2,32,128]{3,1,2,0:T(2,128)S(1)}, u32[]{:S(2)}, u32[]{:S(2)}) %collective-permute-start.4) | collective-permute-done | bytes 65568 | tf_op jit(solution)/shard_map/ppermute | solution.py:175
  40.1 2.4 %collective-permute-start.7 = (f32[2,2,32,128]{3,1,2,0:T(2,128)S(1)}, f32[2,2,32,128]{3,1,2,0:T(2,128)S(1)}, u32[]{:S(2)}, u32[]{:S(2)}) collective-permute-start(f32[2,2,32,128]{3,1,2,0:T(2,128)S(1)} %add.62), channel_id=1, source_target_pairs={{0,64},{16,80},{32,96},{48,112},{64,0},{80,16},{96,32},{112,48},{1... | collective-permute-start | bytes 196616 | tf_op jit(solution)/shard_map/ppermute | solution.py:175
  42.5 5.1 %collective-permute-done.7 = f32[2,2,32,128]{3,1,2,0:T(2,128)S(1)} collective-permute-done((f32[2,2,32,128]{3,1,2,0:T(2,128)S(1)}, f32[2,2,32,128]{3,1,2,0:T(2,128)S(1)}, u32[]{:S(2)}, u32[]{:S(2)}) %collective-permute-start.7) | collective-permute-done | bytes 65568 | tf_op jit(solution)/shard_map/ppermute | solution.py:175
  47.7 1.0 copy-done.2
  48.7 4.8 %shard_map.104 = bf16[16,128,128]{2,1,0:T(8,128)(2,1)S(1)} custom-call(s32[1]{0:T(128)} %bitcast.4.feat_ref, bf16[8,512,128]{2,1,0:T(8,128)(2,1)S(1)} %get-tuple-element.17.own_hbm, bf16[8,1024,128]{2,1,0:T(8,128)(2,1)} %get-tuple-element.18.sides_hbm, bf16[2048,256]{1,0:T(8,128)(2,1)} %collective-permute-done.refs_0_, ...), custom_call_target="tpu_custom_call" | custom-call | flops 1610612736 | bytes 10485760 | tf_op jit(solution)/shard_map/pallas_call | solution.py:128
  53.5 0.8 copy-done.1
  54.3 6.4 %all-to-all-start.1 = ((bf16[16,128,128]{2,1,0:T(8,128)(2,1)}), bf16[16,128,128]{2,1,0:T(8,128)(2,1)S(1)}, u32[]{:S(2)}, u32[]{:S(2)}) async-start(bf16[16,128,128]{2,1,0:T(8,128)(2,1)} %copy-done.1), calls=%async_computation.1 | async-start | bytes 1048576 | tf_op jit(solution)/shard_map/all_to_all | solution.py:272
  60.7 1.2 collective-permute-start.8
  61.9 2.2 %collective-permute-done.8 = f32[2,2,32,128]{3,1,2,0:T(2,128)S(1)} collective-permute-done((f32[2,2,32,128]{3,1,2,0:T(2,128)S(1)}, f32[2,2,32,128]{3,1,2,0:T(2,128)S(1)}, u32[]{:S(2)}, u32[]{:S(2)}) %collective-permute-start.8) | collective-permute-done | bytes 65568 | tf_op jit(solution)/shard_map/ppermute | solution.py:175
  64.2 8.5 %all-to-all-done.1 = bf16[16,128,128]{2,1,0:T(8,128)(2,1)S(1)} async-done(((bf16[16,128,128]{2,1,0:T(8,128)(2,1)}), bf16[16,128,128]{2,1,0:T(8,128)(2,1)S(1)}, u32[]{:S(2)}, u32[]{:S(2)}) %all-to-all-start.1) | async-done | bytes 524320 | tf_op jit(solution)/shard_map/all_to_all | solution.py:272
  72.9 1.2 %pad_maximum_fusion = bf16[8,768,128]{2,1,0:T(8,128)(2,1)} fusion(bf16[8,256,128]{2,1,0:T(8,128)(2,1)S(1)} %broadcast_in_dim.28, bf16[8,512,128]{2,1,0:T(8,128)(2,1)S(1)} %get-tuple-element.17.own_hbm), kind=kLoop, calls=%fused_computation.1 | loop fusion | flops 3145728 | bytes 3145728 | tf_op jit(solution)/shard_map/concatenate | solution.py:287
  74.2 5.9 %all-to-all-start.2 = ((bf16[8,768,128]{2,1,0:T(8,128)(2,1)}), bf16[8,768,128]{2,1,0:T(8,128)(2,1)S(1)}, u32[]{:S(2)}, u32[]{:S(2)}) async-start(bf16[8,768,128]{2,1,0:T(8,128)(2,1)} %pad_maximum_fusion), calls=%async_computation.2 | async-start | bytes 3145728 | tf_op jit(solution)/shard_map/all_to_all | solution.py:287
  80.1 5.0 %collective-permute-start.12 = (bf16[256,256]{1,0:T(8,128)(2,1)S(1)}, bf16[256,256]{1,0:T(8,128)(2,1)S(1)}, u32[]{:S(2)}, u32[]{:S(2)}) collective-permute-start(bf16[256,256]{1,0:T(8,128)(2,1)S(1)} %constant_dynamic-slice_fusion), channel_id=1, source_target_pairs={{0,1},{1,0},{2,3},{3,2},{4,5},{5,4},{6,7},{7,6},{8,9},{9,8},{10,11... | collective-permute-start | bytes 393224 | tf_op jit(solution)/shard_map/ppermute | solution.py:15
  85.1 0.2 fusion.3
  85.4 0.7 collective-permute-done.12
  86.1 0.2 convolution_add_fusion.self_ref
  86.3 2.0 %reduce_sum.51 = bf16[1024,128]{1,0:T(8,128)(2,1)S(1)} reduce(bf16[8,1024,128]{2,1,0:T(8,128)(2,1)} %all-to-all-done, bf16[]{:T(256)} %constant.65.clone.1), dimensions={0}, to_apply=%region_3.4 | reduce | flops 917504 | bytes 2359298 | tf_op jit(solution)/shard_map/reduce_sum | solution.py:277
  88.3 0.7 fusion.18
  89.0 0.6 collective-permute-start.10
  89.6 0.8 collective-permute-start.9
  90.4 5.2 %all-to-all-done.2 = bf16[8,768,128]{2,1,0:T(8,128)(2,1)S(1)} async-done(((bf16[8,768,128]{2,1,0:T(8,128)(2,1)}), bf16[8,768,128]{2,1,0:T(8,128)(2,1)S(1)}, u32[]{:S(2)}, u32[]{:S(2)}) %all-to-all-start.2) | async-done | bytes 1572896 | tf_op jit(solution)/shard_map/all_to_all | solution.py:287
  95.7 0.2 fusion.1
  95.9 6.5 %collective-permute-start.13 = (bf16[8,2,32,128]{3,1,2,0:T(2,128)(2,1)S(1)}, bf16[8,2,32,128]{3,1,2,0:T(2,128)(2,1)S(1)}, u32[]{:S(2)}, u32[]{:S(2)}) collective-permute-start(bf16[8,2,32,128]{3,1,2,0:T(2,128)(2,1)S(1)} %fusion.1), channel_id=1, source_target_pairs={{0,1},{1,0},{2,3},{3,2},{4,5},{5,4},{6,7},{7,6},{8,9},{9,8},{10,11... | collective-permute-start | bytes 393224 | tf_op jit(solution)/shard_map/ppermute | solution.py:15
  102.5 0.8 broadcast_in_dim.29
  103.3 6.9 %all-to-all-start.3 = ((bf16[32,2,16,128]{3,1,2,0:T(2,128)(2,1)}), bf16[32,2,16,128]{3,1,2,0:T(2,128)(2,1)S(1)}, u32[]{:S(2)}, u32[]{:S(2)}) async-start(bf16[32,2,16,128]{3,1,2,0:T(2,128)(2,1)} %bitcast.13), calls=%async_computation.3 | async-start | bytes 524288 | tf_op jit(solution)/shard_map/all_to_all | solution.py:188
  110.2 0.1 convert_reduce_fusion
  110.4 1.0 convert_add_fusion
  111.4 0.4 collective-permute-start.11
  111.8 0.3 broadcast_select_fusion.3
  112.1 0.3 convert_multiply_fusion.2
  112.5 1.0 copy.27
  113.5 1.2 shard_map.105
  114.7 6.4 %all-to-all-done.3 = bf16[32,2,16,128]{3,1,2,0:T(2,128)(2,1)S(1)} async-done(((bf16[32,2,16,128]{3,1,2,0:T(2,128)(2,1)}), bf16[32,2,16,128]{3,1,2,0:T(2,128)(2,1)S(1)}, u32[]{:S(2)}, u32[]{:S(2)}) %all-to-all-start.3) | async-done | bytes 262176 | tf_op jit(solution)/shard_map/all_to_all | solution.py:188
  121.1 0.3 convert_multiply_fusion.1
  121.5 1.0 copy.28
  (47 shorter events, 0.8 us)
Async XLA Ops:
  0.6 23.5 %collective-permute-start.2 = (bf16[2048,256]{1,0:T(8,128)(2,1)}, bf16[2048,256]{1,0:T(8,128)(2,1)}, u32[]{:S(2)}, u32[]{:S(2)}) collective-permute-start(bf16[2048,256]{1,0:T(8,128)(2,1)} %refs_2_.1), channel_id=1, source_target_pairs={{0,1},{1,0},{2,3},{3,2},{4,5},{5,4},{6,7},{7,6},{8,9},{9,8},{10,11... | collective-permute-start | bytes 3145736 | tf_op jit(solution)/shard_map/ppermute | solution.py:15
  1.4 25.2 %collective-permute-start = (bf16[2048,256]{1,0:T(8,128)(2,1)}, bf16[2048,256]{1,0:T(8,128)(2,1)}, u32[]{:S(2)}, u32[]{:S(2)}) collective-permute-start(bf16[2048,256]{1,0:T(8,128)(2,1)} %refs_2_.1), channel_id=1, source_target_pairs={{0,16},{16,32},{32,48},{48,64},{64,80},{80,96},{96,112},{112,128},... | collective-permute-start | bytes 3145736 | tf_op jit(solution)/shard_map/ppermute | solution.py:15
  3.0 25.1 %collective-permute-start.1 = (bf16[2048,256]{1,0:T(8,128)(2,1)}, bf16[2048,256]{1,0:T(8,128)(2,1)}, u32[]{:S(2)}, u32[]{:S(2)}) collective-permute-start(bf16[2048,256]{1,0:T(8,128)(2,1)} %refs_2_.1), channel_id=1, source_target_pairs={{0,240},{16,0},{32,16},{48,32},{64,48},{80,64},{96,80},{112,96},{1... | collective-permute-start | bytes 3145736 | tf_op jit(solution)/shard_map/ppermute | solution.py:15
  3.1 2.1 %copy-start.5 = (s32[16,16]{1,0:T(8,128)S(1)}, s32[16,16]{1,0:T(8,128)}, u32[]{:S(2)}) copy-start(s32[16,16]{1,0:T(8,128)} %param.11) | copy-start | bytes 3076
  3.1 2.1 %copy-start.6 = (s32[16]{0:T(128)S(1)}, s32[16]{0:T(128)}, u32[]{:S(2)}) copy-start(s32[16]{0:T(128)} %param.12) | copy-start | bytes 196
  16.8 6.8 %copy-start = (bf16[2048,256]{1,0:T(8,128)(2,1)S(1)}, bf16[2048,256]{1,0:T(8,128)(2,1)}, u32[]{:S(2)}) copy-start(bf16[2048,256]{1,0:T(8,128)(2,1)} %refs_2_.1) | copy-start | bytes 3145732
  16.8 37.5 %all-to-all-start = ((bf16[8,1024,128]{2,1,0:T(8,128)(2,1)}), bf16[8,1024,128]{2,1,0:T(8,128)(2,1)}, u32[]{:S(2)}, u32[]{:S(2)}) async-start(bf16[8,1024,128]{2,1,0:T(8,128)(2,1)} %get-tuple-element.18.sides_hbm), calls=%async_computation | async-start | bytes 4194304 | tf_op jit(solution)/shard_map/all_to_all | solution.py:241
  28.2 19.5 %collective-permute-start.5 = (bf16[2048,256]{1,0:T(8,128)(2,1)}, bf16[2048,256]{1,0:T(8,128)(2,1)S(1)}, u32[]{:S(2)}, u32[]{:S(2)}) collective-permute-start(bf16[2048,256]{1,0:T(8,128)(2,1)} %collective-permute-done.refs_0_), channel_id=1, source_target_pairs={{0,1},{1,0},{2,3},{3,2},{4,5},{5,4},{6,7},{7,6},{8,9},{9,8},{10,11... | collective-permute-start | bytes 3145736 | tf_op jit(solution)/shard_map/ppermute | solution.py:15
  29.1 18.5 %collective-permute-start.6 = (bf16[2048,256]{1,0:T(8,128)(2,1)}, bf16[2048,256]{1,0:T(8,128)(2,1)S(1)}, u32[]{:S(2)}, u32[]{:S(2)}) collective-permute-start(bf16[2048,256]{1,0:T(8,128)(2,1)} %collective-permute-done.1.refs_4_), channel_id=1, source_target_pairs={{0,1},{1,0},{2,3},{3,2},{4,5},{5,4},{6,7},{7,6},{8,9},{9,8},{10,11... | collective-permute-start | bytes 3145736 | tf_op jit(solution)/shard_map/ppermute | solution.py:15
  29.1 5.2 %collective-permute-start.3 = (f32[2,2,32,128]{3,1,2,0:T(2,128)S(1)}, f32[2,2,32,128]{3,1,2,0:T(2,128)S(1)}, u32[]{:S(2)}, u32[]{:S(2)}) collective-permute-start(f32[2,2,32,128]{3,1,2,0:T(2,128)S(1)} %pad_maximum_fusion.1), channel_id=1, source_target_pairs={{0,16},{16,0},{32,48},{48,32},{64,80},{80,64},{96,112},{112,96},{1... | collective-permute-start | bytes 196616 | tf_op jit(solution)/shard_map/ppermute | solution.py:175
  34.4 5.6 %collective-permute-start.4 = (f32[2,2,32,128]{3,1,2,0:T(2,128)S(1)}, f32[2,2,32,128]{3,1,2,0:T(2,128)S(1)}, u32[]{:S(2)}, u32[]{:S(2)}) collective-permute-start(f32[2,2,32,128]{3,1,2,0:T(2,128)S(1)} %add.61), channel_id=1, source_target_pairs={{0,32},{16,48},{32,0},{48,16},{64,96},{80,112},{96,64},{112,80},{1... | collective-permute-start | bytes 196616 | tf_op jit(solution)/shard_map/ppermute | solution.py:175
  40.1 7.5 %collective-permute-start.7 = (f32[2,2,32,128]{3,1,2,0:T(2,128)S(1)}, f32[2,2,32,128]{3,1,2,0:T(2,128)S(1)}, u32[]{:S(2)}, u32[]{:S(2)}) collective-permute-start(f32[2,2,32,128]{3,1,2,0:T(2,128)S(1)} %add.62), channel_id=1, source_target_pairs={{0,64},{16,80},{32,96},{48,112},{64,0},{80,16},{96,32},{112,48},{1... | collective-permute-start | bytes 196616 | tf_op jit(solution)/shard_map/ppermute | solution.py:175
  47.7 1.1 copy-start.2
  53.5 0.8 copy-start.1
  54.3 18.4 %all-to-all-start.1 = ((bf16[16,128,128]{2,1,0:T(8,128)(2,1)}), bf16[16,128,128]{2,1,0:T(8,128)(2,1)S(1)}, u32[]{:S(2)}, u32[]{:S(2)}) async-start(bf16[16,128,128]{2,1,0:T(8,128)(2,1)} %copy-done.1), calls=%async_computation.1 | async-start | bytes 1048576 | tf_op jit(solution)/shard_map/all_to_all | solution.py:272
  60.7 3.4 %collective-permute-start.8 = (f32[2,2,32,128]{3,1,2,0:T(2,128)S(1)}, f32[2,2,32,128]{3,1,2,0:T(2,128)S(1)}, u32[]{:S(2)}, u32[]{:S(2)}) collective-permute-start(f32[2,2,32,128]{3,1,2,0:T(2,128)S(1)} %add.63), channel_id=1, source_target_pairs={{0,128},{16,144},{32,160},{48,176},{64,192},{80,208},{96,224},{112... | collective-permute-start | bytes 196616 | tf_op jit(solution)/shard_map/ppermute | solution.py:175
  74.1 11.0 %copy-start.4 = (bf16[256,512]{1,0:T(8,128)(2,1)S(1)}, bf16[256,512]{1,0:T(8,128)(2,1)}, u32[]{:S(2)}) copy-start(bf16[256,512]{1,0:T(8,128)(2,1)} %param.14) | copy-start | bytes 786436
  74.1 11.2 %copy-start.3 = (bf16[256,512]{1,0:T(8,128)(2,1)S(1)}, bf16[256,512]{1,0:T(8,128)(2,1)}, u32[]{:S(2)}) copy-start(bf16[256,512]{1,0:T(8,128)(2,1)} %param.15) | copy-start | bytes 786436
  74.2 21.5 %all-to-all-start.2 = ((bf16[8,768,128]{2,1,0:T(8,128)(2,1)}), bf16[8,768,128]{2,1,0:T(8,128)(2,1)S(1)}, u32[]{:S(2)}, u32[]{:S(2)}) async-start(bf16[8,768,128]{2,1,0:T(8,128)(2,1)} %pad_maximum_fusion), calls=%async_computation.2 | async-start | bytes 3145728 | tf_op jit(solution)/shard_map/all_to_all | solution.py:287
  80.1 6.0 %collective-permute-start.12 = (bf16[256,256]{1,0:T(8,128)(2,1)S(1)}, bf16[256,256]{1,0:T(8,128)(2,1)S(1)}, u32[]{:S(2)}, u32[]{:S(2)}) collective-permute-start(bf16[256,256]{1,0:T(8,128)(2,1)S(1)} %constant_dynamic-slice_fusion), channel_id=1, source_target_pairs={{0,1},{1,0},{2,3},{3,2},{4,5},{5,4},{6,7},{7,6},{8,9},{9,8},{10,11... | collective-permute-start | bytes 393224 | tf_op jit(solution)/shard_map/ppermute | solution.py:15
  89.0 21.4 %collective-permute-start.10 = (bf16[512,128]{1,0:T(8,128)(2,1)}, bf16[512,128]{1,0:T(8,128)(2,1)}, u32[]{:S(2)}, u32[]{:S(2)}) collective-permute-start(bf16[512,128]{1,0:T(8,128)(2,1)} %get-tuple-element.40), channel_id=1, source_target_pairs={{0,16},{16,32},{32,48},{48,64},{64,80},{80,96},{96,112},{112,128},... | collective-permute-start | bytes 393224 | tf_op jit(solution)/shard_map/ppermute | solution.py:15
  89.6 20.7 %collective-permute-start.9 = (bf16[512,128]{1,0:T(8,128)(2,1)S(1)}, bf16[512,128]{1,0:T(8,128)(2,1)}, u32[]{:S(2)}, u32[]{:S(2)}) collective-permute-start(bf16[512,128]{1,0:T(8,128)(2,1)S(1)} %get-tuple-element.39), channel_id=1, source_target_pairs={{0,240},{16,0},{32,16},{48,32},{64,48},{80,64},{96,80},{112,96},{1... | collective-permute-start | bytes 393224 | tf_op jit(solution)/shard_map/ppermute | solution.py:15
  95.9 15.9 %collective-permute-start.13 = (bf16[8,2,32,128]{3,1,2,0:T(2,128)(2,1)S(1)}, bf16[8,2,32,128]{3,1,2,0:T(2,128)(2,1)S(1)}, u32[]{:S(2)}, u32[]{:S(2)}) collective-permute-start(bf16[8,2,32,128]{3,1,2,0:T(2,128)(2,1)S(1)} %fusion.1), channel_id=1, source_target_pairs={{0,1},{1,0},{2,3},{3,2},{4,5},{5,4},{6,7},{7,6},{8,9},{9,8},{10,11... | collective-permute-start | bytes 393224 | tf_op jit(solution)/shard_map/ppermute | solution.py:15
  103.3 17.8 %all-to-all-start.3 = ((bf16[32,2,16,128]{3,1,2,0:T(2,128)(2,1)}), bf16[32,2,16,128]{3,1,2,0:T(2,128)(2,1)S(1)}, u32[]{:S(2)}, u32[]{:S(2)}) async-start(bf16[32,2,16,128]{3,1,2,0:T(2,128)(2,1)} %bitcast.13), calls=%async_computation.3 | async-start | bytes 524288 | tf_op jit(solution)/shard_map/all_to_all | solution.py:188
  111.4 2.2 %collective-permute-start.11 = (f32[2,256,128]{2,1,0:T(8,128)S(1)}, f32[2,256,128]{2,1,0:T(8,128)S(1)}, u32[]{:S(2)}, u32[]{:S(2)}) collective-permute-start(f32[2,256,128]{2,1,0:T(8,128)S(1)} %bitcast.43), channel_id=1, source_target_pairs={{0,1},{1,0},{2,3},{3,2},{4,5},{5,4},{6,7},{7,6},{8,9},{9,8},{10,11... | collective-permute-start | bytes 786440 | tf_op jit(solution)/shard_map/ppermute | solution.py:15
